TPU v7x, 256 devices: a whole 4x4x8 slice. The times are simulated.
256 devices in a mesh: prompt: 8 (over z), group: 8 (over x, core), tensor: 4 (over y).
Axes of the slice: x: 4, y: 4, z: 8, core: 2. Of those that a mesh axis runs over, the one named last changes fastest.
Arguments:
- prompt_q: bfloat16 [8192, 3584], P(('prompt', 'group'), 'tensor'), parts along dimension 0, may hold values from -8 to 8
- prefix_kv: bfloat16 [2, 8192, 512], P(None, ('prompt', 'group', 'tensor')), parts along dimension 1, may hold values from -16 to 16
- resp_q: bfloat16 [16384, 3584], P(('prompt', 'group'), 'tensor'), parts along dimension 0, may hold values from -8 to 8
- resp_kv: bfloat16 [2, 16384, 512], P(None, ('prompt', 'group'), 'tensor'), parts along dimension 1, may hold values from -4 to 4
- resp_segs: int32 [16384], P('prompt'), parts along dimension 0, may hold values from 0 to 31, as said below
- grad_prompt_out: bfloat16 [8192, 3584], P(('prompt', 'group'), 'tensor'), parts along dimension 0, may hold values from -4 to 4
- grad_resp_out: bfloat16 [16384, 3584], P(('prompt', 'group'), 'tensor'), parts along dimension 0, may hold values from -4 to 4
Outputs:
- prompt_out: bfloat16 [8192, 3584], P(('prompt', 'group'), 'tensor'), parts along dimension 0
- resp_out: bfloat16 [16384, 3584], P(('prompt', 'group'), 'tensor'), parts along dimension 0
- grad_prompt_q: bfloat16 [8192, 3584], P(('prompt', 'group'), 'tensor'), parts along dimension 0
- grad_resp_q: bfloat16 [16384, 3584], P(('prompt', 'group'), 'tensor'), parts along dimension 0
- grad_prefix_kv: bfloat16 [2, 8192, 512], P(None, ('prompt', 'group', 'tensor')), parts along dimension 1
- grad_resp_kv: bfloat16 [2, 16384, 512], P(None, ('prompt', 'group'), 'tensor'), parts along dimension 1
There are 8 independent parts, one for each index of `prompt`. A program takes and returns all parts, laid end to end along the dimension named above; each array names one. Nothing has to cross between parts.
Inputs may be any that keep to these rules, and one draw needn't show every extreme that they name: `resp_segs`: row 0 holds 0; the numbers never fall and grow by one where a response starts. A response starts at row 0 and at every row equal to half of 128 plus a multiple of 128; between each two such rows after the first two, and after the last of them, exactly one more response starts. Every response has 1 to 128 rows; the one that starts at half of 128 has exactly 128.
All inputs are finite; a program needn't handle non-finite values.
Results may differ from a plain program's by a relative error of at most 0.02.
Values may be sent and summed in bfloat16 or wider, within the bound.
No kernel may reach another device: no remote copies, remote signals or barrier semaphores. Data moves between devices by JAX's collectives and lax.ppermute only.
A program may use at most 64 MiB of HBM per device.

v0:
```python
import math

import jax
import jax.numpy as jnp
from jax import lax
from jax.sharding import PartitionSpec as P

HEAD_DIM = 128


def shifted(array, axis, by):
    count = lax.axis_size(axis)
    pairs = [(i, i + by) for i in range(count) if 0 <= i + by < count]
    return lax.ppermute(array, axis, pairs)


def fetch_block(source, block_id):
    key_all, value_all, span_rows, block_count, masker = source
    start_row = block_id * span_rows
    key_rows = lax.dynamic_slice_in_dim(key_all, start_row, span_rows, 0)
    value_rows = lax.dynamic_slice_in_dim(value_all, start_row, span_rows, 0)
    return (key_rows, value_rows, masker(start_row), start_row)


def block_scores(queries, key_rows, visible, score_scale):
    scores = (
        jnp.einsum("qd,kd->qk", queries, key_rows, preferred_element_type=jnp.float32) * score_scale
    )
    if visible is None:
        return scores
    return jnp.where(visible, scores, -jnp.inf)


def block_weights(queries, key_rows, visible, score_scale, row_peak, row_total):
    scores = block_scores(queries, key_rows, visible, score_scale)
    return (jnp.exp(scores - row_peak) / row_total).astype(jnp.bfloat16)


def softmax_stats(queries, sources, score_scale):
    height = queries.shape[0]
    running = (jnp.full((height, 1), -1e30, jnp.float32), jnp.zeros((height, 1), jnp.float32))
    for source in sources:

        def advance(block_id, carried, source=source):
            row_peak, row_total = carried
            key_rows, value_rows, visible, start_row = fetch_block(source, block_id)
            scores = block_scores(queries, key_rows, visible, score_scale)
            new_peak = jnp.maximum(row_peak, jnp.max(scores, axis=1, keepdims=True))
            row_total = row_total * jnp.exp(row_peak - new_peak) + jnp.sum(
                jnp.exp(scores - new_peak), axis=1, keepdims=True
            )
            return (new_peak, row_total)

        running = lax.fori_loop(0, source[3], advance, running)
    return running


def attend_values(queries, sources, score_scale, row_peak, row_total):
    mixed = jnp.zeros((queries.shape[0], HEAD_DIM), jnp.float32)
    for source in sources:

        def accumulate(block_id, mixed, source=source):
            key_rows, value_rows, visible, start_row = fetch_block(source, block_id)
            weights = block_weights(queries, key_rows, visible, score_scale, row_peak, row_total)
            return mixed + jnp.dot(weights, value_rows, preferred_element_type=jnp.float32)

        mixed = lax.fori_loop(0, source[3], accumulate, mixed)
    return mixed.astype(jnp.bfloat16)


def attend_grads(queries, upstream, outputs, sources, score_scale, row_peak, row_total):
    row_delta = jnp.sum(
        upstream.astype(jnp.float32) * outputs.astype(jnp.float32), axis=1, keepdims=True
    )
    grad_query = jnp.zeros((queries.shape[0], HEAD_DIM), jnp.float32)
    kv_terms = []
    for source in sources:

        def backprop(block_id, carried, source=source):
            grad_query, grad_key, grad_value = carried
            key_rows, value_rows, visible, start_row = fetch_block(source, block_id)
            span_rows = source[2]
            weights = block_weights(queries, key_rows, visible, score_scale, row_peak, row_total)
            grad_prob = jnp.einsum(
                "qd,kd->qk", upstream, value_rows, preferred_element_type=jnp.float32
            )
            dscore = (weights.astype(jnp.float32) * (grad_prob - row_delta)).astype(jnp.bfloat16)
            grad_query = grad_query + jnp.dot(dscore, key_rows, preferred_element_type=jnp.float32)
            key_term = jnp.einsum("qk,qd->kd", dscore, queries, preferred_element_type=jnp.float32)
            value_term = jnp.einsum(
                "qk,qd->kd", weights, upstream, preferred_element_type=jnp.float32
            )
            grad_key = lax.dynamic_update_slice_in_dim(
                grad_key,
                lax.dynamic_slice_in_dim(grad_key, start_row, span_rows, 0) + key_term,
                start_row,
                0,
            )
            grad_value = lax.dynamic_update_slice_in_dim(
                grad_value,
                lax.dynamic_slice_in_dim(grad_value, start_row, span_rows, 0) + value_term,
                start_row,
                0,
            )
            return (grad_query, grad_key, grad_value)

        zero_rows = jnp.zeros(source[0].shape, jnp.float32)
        grad_query, grad_key, grad_value = lax.fori_loop(
            0, source[3], backprop, (grad_query, zero_rows, zero_rows)
        )
        kv_terms.append((grad_key, grad_value))
    return (grad_query, kv_terms)


def attend(queries, upstream, sources, score_scale):
    row_peak, row_total = softmax_stats(queries, sources, score_scale)
    outputs = attend_values(queries, sources, score_scale, row_peak, row_total)
    grad_query, kv_terms = attend_grads(
        queries, upstream, outputs, sources, score_scale, row_peak, row_total
    )
    return (outputs, grad_query * score_scale, kv_terms)


def prompt_pass(rows_q, rows_up, first_row, prefix_keys, prefix_values, key_block, score_scale):
    height = rows_q.shape[0]
    local_heads = rows_q.shape[1] // HEAD_DIM
    queries = rows_q.reshape(height * local_heads, HEAD_DIM)
    upstream = rows_up.reshape(height * local_heads, HEAD_DIM)
    positions = first_row + jnp.arange(height * local_heads, dtype=jnp.int32) // local_heads
    block_count = (first_row + height - 1) // key_block + 1

    def causal(start_row):
        return (start_row + jnp.arange(key_block, dtype=jnp.int32))[None, :] <= positions[:, None]

    sources = [(prefix_keys, prefix_values, key_block, block_count, causal)]
    outputs, grad_query, kv_terms = attend(queries, upstream, sources, score_scale)
    return (
        outputs.reshape(height, local_heads * HEAD_DIM),
        grad_query.astype(jnp.bfloat16).reshape(height, local_heads * HEAD_DIM),
        kv_terms[0],
    )


def local(prompt_q, prefix_kv, resp_q, resp_kv, resp_segs, grad_prompt_out, grad_resp_out):
    score_scale = HEAD_DIM ** (-0.5)
    prompt_dev = prompt_q.shape[0]
    resp_dev = resp_q.shape[0]
    local_heads = resp_q.shape[1] // HEAD_DIM
    group_size = lax.axis_size("group")
    tensor_size = lax.axis_size("tensor")
    group_rank = lax.axis_index("group")
    tensor_rank = lax.axis_index("tensor")
    prompt_len = prompt_dev * group_size
    key_block = math.gcd(256, prompt_len)
    earlier_kv = shifted(resp_kv, "group", 1)
    all_heads = lax.all_gather(prefix_kv, ("group", "tensor"), axis=1, tiled=True)
    prefix_own = lax.dynamic_slice_in_dim(all_heads, tensor_rank * HEAD_DIM, HEAD_DIM, 2)
    prefix_keys = prefix_own[0]
    prefix_values = prefix_own[1]
    own_segs = lax.dynamic_slice_in_dim(resp_segs, group_rank * resp_dev, resp_dev)
    prior_segs = lax.dynamic_slice_in_dim(
        resp_segs, jnp.maximum(group_rank - 1, 0) * resp_dev, resp_dev
    )
    prior_segs = jnp.where(group_rank > 0, prior_segs, -1)
    query_segs = jnp.repeat(own_segs, local_heads)
    query_rows = jnp.repeat(jnp.arange(resp_dev, dtype=jnp.int32), local_heads)

    def from_prior(start_row):
        return prior_segs[None, :] == query_segs[:, None]

    def from_self(start_row):
        return (own_segs[None, :] == query_segs[:, None]) & (
            jnp.arange(resp_dev, dtype=jnp.int32)[None, :] <= query_rows[:, None]
        )

    def from_prefix(start_row):
        return None

    resp_sources = [
        (earlier_kv[0], earlier_kv[1], resp_dev, 1, from_prior),
        (resp_kv[0], resp_kv[1], resp_dev, 1, from_self),
        (prefix_keys, prefix_values, key_block, prompt_len // key_block, from_prefix),
    ]
    resp_queries = resp_q.reshape(resp_dev * local_heads, HEAD_DIM)
    resp_upstream = grad_resp_out.reshape(resp_dev * local_heads, HEAD_DIM)
    resp_outputs, resp_grad_q, resp_terms = attend(
        resp_queries, resp_upstream, resp_sources, score_scale
    )
    resp_out = resp_outputs.reshape(resp_dev, local_heads * HEAD_DIM)
    grad_resp_q = resp_grad_q.astype(jnp.bfloat16).reshape(resp_dev, local_heads * HEAD_DIM)
    prior_grads = jnp.stack((resp_terms[0][0] * score_scale, resp_terms[0][1]))
    later_grads = shifted(prior_grads.astype(jnp.bfloat16), "group", -1).astype(prior_grads.dtype)
    grad_resp_kv = (
        jnp.stack((resp_terms[1][0] * score_scale, resp_terms[1][1])) + later_grads
    ).astype(jnp.bfloat16)
    prompt_out, grad_prompt_q, own_terms = prompt_pass(
        prompt_q,
        grad_prompt_out,
        group_rank * prompt_dev,
        prefix_keys,
        prefix_values,
        key_block,
        score_scale,
    )
    prompt_key_grad = own_terms[0]
    prompt_value_grad = own_terms[1]
    prefix_key_total = (prompt_key_grad + resp_terms[2][0]) * score_scale
    prefix_value_total = prompt_value_grad + resp_terms[2][1]
    partial_kv = jnp.stack((prefix_key_total, prefix_value_total))
    cache_rows = prompt_len // (group_size * tensor_size)
    arranged = partial_kv.reshape(2, group_size, tensor_size, cache_rows, HEAD_DIM)
    regrouped = lax.all_to_all(
        arranged.astype(jnp.bfloat16), "tensor", split_axis=2, concat_axis=4, tiled=True
    ).astype(arranged.dtype)
    regrouped = regrouped.reshape(2, group_size, cache_rows, tensor_size * HEAD_DIM)
    summed = lax.psum_scatter(
        regrouped.astype(jnp.bfloat16), "group", scatter_dimension=1, tiled=True
    ).astype(jnp.float32)
    grad_prefix_kv = summed.reshape(2, cache_rows, tensor_size * HEAD_DIM).astype(jnp.bfloat16)
    return (prompt_out, resp_out, grad_prompt_q, grad_resp_q, grad_prefix_kv, grad_resp_kv)


def solution(mesh):
    in_specs = (
        P(("prompt", "group"), "tensor"),
        P(None, ("prompt", "group", "tensor"), None),
        P(("prompt", "group"), "tensor"),
        P(None, ("prompt", "group"), "tensor"),
        P("prompt"),
        P(("prompt", "group"), "tensor"),
        P(("prompt", "group"), "tensor"),
    )
    out_specs = (
        P(("prompt", "group"), "tensor"),
        P(("prompt", "group"), "tensor"),
        P(("prompt", "group"), "tensor"),
        P(("prompt", "group"), "tensor"),
        P(None, ("prompt", "group", "tensor"), None),
        P(None, ("prompt", "group"), "tensor"),
    )
    return jax.shard_map(local, mesh=mesh, in_specs=in_specs, out_specs=out_specs, check_vma=False)
```

profile of v0, /device:TPU:1, one launch (start us, length us, event | category | flops | bytes accessed | tf_op | source)
XLA Modules:
  0.0 255.2 jit_solution(7896597058583364701)
XLA Ops:
  7.9 4.5 %collective-permute-start = (bf16[2,256,128]{2,1,0:T(8,128)(2,1)}, bf16[2,256,128]{2,1,0:T(8,128)(2,1)S(1)}, u32[]{:S(2)}, u32[]{:S(2)}) collective-permute-start(bf16[2,256,128]{2,1,0:T(8,128)(2,1)} %param.22), channel_id=1, source_target_pairs={{0,4},{4,8},{8,12},{12,16},{16,20},{20,24},{24,28},{1,5},{5,9},{9,... | collective-permute-start | bytes 393224 | tf_op jit(solution)/shard_map/ppermute | solution.py:14
  13.6 1.5 reshape.140
  15.3 2.7 %fusion.118 = (f32[1792]{0:T(1024)S(1)}, f32[1792,256]{0,1:T(8,128)}) fusion(bf16[1792,128]{1,0:T(8,128)(2,1)S(1)} %reshape.140, bf16[2,256,128]{2,1,0:T(8,128)(2,1)} %param.22, s32[1792]{0:T(1024)S(1)} %le.90, s32[1792]{0:T(1024)S(1)} %eq.97, s32[256]{0:T(256)S(1)} %get-tuple-element.976), kind=kOutput, calls=%fused_computation.180 | convolution fusion | flops 120191232 | bytes 2381824 | tf_op jit(solution)/shard_map/while/body/eval_jaxpr/qd,kd->qk/dot_general | solution.py:27
  20.2 2.7 %exponential_reduce_fusion.2 = (f32[1792]{0:T(1024)S(1)}, f32[1792]{0:T(1024)S(1)}) fusion(f32[1792,256]{0,1:T(8,128)} %get-tuple-element.980, f32[1792]{0:T(1024)S(1)} %get-tuple-element.974, f32[1792,256]{0,1:T(8,128)S(1)} %get-tuple-element.978, f32[1792]{0:T(1024)S(1)} %get-tuple-element.973), kind=kLoop, calls=%fused_computation.133 | loop fusion | flops 1831424 | bytes 3698688 | tf_op jit(solution)/shard_map/while/body/eval_jaxpr/reduce_sum | solution.py:49
  22.9 40.9 %all-gather.2.cloned.1.call-done = bf16[2,1024,512]{2,1,0:T(8,128)(2,1)} async-done(((bf16[2,32,512]{2,1,0:T(8,128)(2,1)}), bf16[2,1024,512]{2,1,0:T(8,128)(2,1)}) %all-gather.2.cloned.1.call-update) | async-done | bytes 2097168 | tf_op jit(solution)/shard_map/all_gather | solution.py:156
  63.8 1.8 dynamic-slice_bitcast_fusion
  65.5 3.1 %while.21 = (s32[]{:T(128)}, f32[1792,1]{0,1:T(1,128)S(1)}, f32[1792,1]{0,1:T(1,128)S(1)}, bf16[1024,128]{1,0:T(8,128)(2,1)S(1)}, bf16[1792,128]{1,0:T(8,128)(2,...) while((s32[]{:T(128)}, f32[1792,1]{0,1:T(1,128)S(1)}, f32[1792,1]{0,1:T(1,128)S(1)}, ...), condition=%wide.region_13.14_spmd, body=%wide.region_10.13_spmd.sunk | while | flops 119279112 | bytes 4294799 | solution.py:54
  68.8 2.6 %divide_convert_fusion.1 = (bf16[1792,256]{0,1:T(8,128)(2,1)S(1)}, bf16[1792,256]{0,1:T(8,128)(2,1)S(1)}) fusion(f32[1792,256]{0,1:T(8,128)} %copy-done.2, f32[1792]{0:T(1024)S(1)} %reduce.15, f32[1792]{0:T(1024)S(1)} %reduce.14, f32[1792,256]{0,1:T(8,128)} %get-tuple-element.980), kind=kLoop, calls=%fused_computation.132 | loop fusion | flops 2752512 | bytes 5519360 | tf_op jit(solution)/shard_map/while/body/eval_jaxpr/convert_element_type | solution.py:36
  72.5 1.4 convolution_add_fusion.8
  73.9 12.1 %while.22 = (s32[]{:T(128)}, f32[1792,128]{1,0:T(8,128)}, bf16[1024,128]{1,0:T(8,128)(2,1)S(1)}, bf16[1792,128]{1,0:T(8,128)(2,1)S(1)}, f32[1792,1]{0,1:T(1,128)...) while((s32[]{:T(128)}, f32[1792,128]{1,0:T(8,128)}, ...), condition=%wide.region_15.16_spmd, body=%wide.region_14.15_spmd.sunk | while | flops 236945408 | bytes 2471083 | solution.py:67
  73.9 3.0 %convolution_add_fusion.12 = f32[1792,128]{1,0:T(8,128)} fusion(f32[1792,128]{1,0:T(8,128)} %get-tuple-element.1435, bf16[1792,128]{1,0:T(8,128)(2,1)S(1)} %get-tuple-element.1449, f32[1792]{0:T(1024)S(1)} %reduce.31, f32[1792]{0:T(1024)S(1)} %reduce.32, bf16[1024,128]{1,0:T(8,128)(2,1)} %get-tuple-element.1452, s32[]{:T(128)S(6)} %select_n.195, ...), kind=kOutput, calls=%fused_computation.14.clone.1 | convolution fusion | flops 236945408 | bytes 2442240 | tf_op jit(solution)/shard_map/while/body/eval_jaxpr/dot_general | solution.py:65
  77.0 3.0 %convolution_add_fusion.12 = f32[1792,128]{1,0:T(8,128)} fusion(f32[1792,128]{1,0:T(8,128)} %get-tuple-element.1435, bf16[1792,128]{1,0:T(8,128)(2,1)S(1)} %get-tuple-element.1449, f32[1792]{0:T(1024)S(1)} %reduce.31, f32[1792]{0:T(1024)S(1)} %reduce.32, bf16[1024,128]{1,0:T(8,128)(2,1)} %get-tuple-element.1452, s32[]{:T(128)S(6)} %select_n.195, ...), kind=kOutput, calls=%fused_computation.14.clone.1 | convolution fusion | flops 236945408 | bytes 2442240 | tf_op jit(solution)/shard_map/while/body/eval_jaxpr/dot_general | solution.py:65
  80.0 3.0 %convolution_add_fusion.12 = f32[1792,128]{1,0:T(8,128)} fusion(f32[1792,128]{1,0:T(8,128)} %get-tuple-element.1435, bf16[1792,128]{1,0:T(8,128)(2,1)S(1)} %get-tuple-element.1449, f32[1792]{0:T(1024)S(1)} %reduce.31, f32[1792]{0:T(1024)S(1)} %reduce.32, bf16[1024,128]{1,0:T(8,128)(2,1)} %get-tuple-element.1452, s32[]{:T(128)S(6)} %select_n.195, ...), kind=kOutput, calls=%fused_computation.14.clone.1 | convolution fusion | flops 236945408 | bytes 2442240 | tf_op jit(solution)/shard_map/while/body/eval_jaxpr/dot_general | solution.py:65
  83.0 3.0 %convolution_add_fusion.12 = f32[1792,128]{1,0:T(8,128)} fusion(f32[1792,128]{1,0:T(8,128)} %get-tuple-element.1435, bf16[1792,128]{1,0:T(8,128)(2,1)S(1)} %get-tuple-element.1449, f32[1792]{0:T(1024)S(1)} %reduce.31, f32[1792]{0:T(1024)S(1)} %reduce.32, bf16[1024,128]{1,0:T(8,128)(2,1)} %get-tuple-element.1452, s32[]{:T(128)S(6)} %select_n.195, ...), kind=kOutput, calls=%fused_computation.14.clone.1 | convolution fusion | flops 236945408 | bytes 2442240 | tf_op jit(solution)/shard_map/while/body/eval_jaxpr/dot_general | solution.py:65
  87.2 1.0 multiply_reduce_fusion
  88.6 1.0 fusion.97
  91.6 2.1 collective-permute-start.1
  95.8 25.3 %while.23 = (s32[]{:T(128)}, f32[1792,128]{1,0:T(8,128)S(1)}, f32[1024,128]{1,0:T(8,128)}, f32[1024,128]{1,0:T(8,128)}, bf16[1024,128]{1,0:T(8,128)(2,1)S(1)}, /...) while((s32[]{:T(128)}, f32[1792,128]{1,0:T(8,128)S(1)}, ...), condition=%wide.region_21.22_spmd, body=%wide.region_20.21_spmd.sunk | while | flops 591167488 | bytes 9962723 | solution.py:108
  96.4 1.3 fusion.214
  98.3 2.0 fusion.215
  100.2 1.9 fusion.216
  102.8 1.3 fusion.214
  104.6 2.0 fusion.215
  106.6 1.9 fusion.216
  109.1 1.2 fusion.214
  110.9 1.9 fusion.215
  112.9 1.9 fusion.216
  115.4 1.2 fusion.214
  117.3 1.9 fusion.215
  119.2 1.9 fusion.216
  122.0 1.6 while.25
  122.1 1.5 fusion.225
  126.1 8.1 %while.26 = (s32[]{:T(128)}, f32[896,128]{1,0:T(8,128)S(1)}, f32[1024,128]{1,0:T(8,128)}, f32[1024,128]{1,0:T(8,128)}, s32[]{:T(128)}, /*index=5*/bf16[1024,128]...) while((s32[]{:T(128)}, f32[896,128]{1,0:T(8,128)S(1)}, ...), condition=%wide.region_18.19_spmd.clone, body=%wide.region_17.18_spmd.clone.sunk | while | flops 296083584 | bytes 5350651 | solution.py:108
  127.9 1.1 fusion.237
  129.0 1.1 fusion.238
  130.2 1.9 fusion.239
  132.4 1.8 fusion.240
  134.2 1.1 multiply_convert_fusion.1
  135.4 1.3 add_convert_fusion
  137.5 3.5 %all-to-all-start = ((bf16[2,8,4,32,128]{4,3,0,1,2:T(8,128)(2,1)}), bf16[2,8,4,32,128]{4,3,0,1,2:T(8,128)(2,1)S(1)}, u32[]{:S(2)}, u32[]{:S(2)}) async-start(bf16[2,8,4,32,128]{4,3,0,1,2:T(8,128)(2,1)} %copy.29), calls=%async_computation | async-start | bytes 1048576 | tf_op jit(solution)/shard_map/all_to_all | solution.py:212
  141.9 9.1 %all-to-all-done = bf16[2,8,4,32,128]{4,3,0,1,2:T(8,128)(2,1)S(1)} async-done(((bf16[2,8,4,32,128]{4,3,0,1,2:T(8,128)(2,1)}), bf16[2,8,4,32,128]{4,3,0,1,2:T(8,128)(2,1)S(1)}, u32[]{:S(2)}, u32[]{:S(2)}) %all-to-all-start) | async-done | bytes 524320 | tf_op jit(solution)/shard_map/all_to_all | solution.py:212
  151.4 1.0 all_to_all.16
  152.9 1.2 reshape.145
  154.1 1.2 reshape.141
  155.3 0.9 reshape.143
  157.2 1.6 fusion.101
  158.8 87.4 %all-reduce.3.cloned.1.call-done = bf16[2,8,32,512]{3,2,1,0:T(8,128)(2,1)} async-done(((bf16[2,8,32,512]{3,2,1,0:T(8,128)(2,1)}), bf16[2,8,32,512]{3,2,1,0:T(8,128)(2,1)}) %all-reduce.3.cloned.1.call-update) | async-done | bytes 524304
  246.2 2.2 dynamic-slice_bitcast_fusion.2
  (148 shorter events, 28.2 us)
Async XLA Ops:
  7.2 56.6 %all-gather.2.cloned.1.call-start = ((), (), s32[]{:S(2)}) async-start(), calls=%async_computation.1 | async-start | bytes 2162688 | tf_op jit(solution)/shard_map/all_gather | solution.py:156
  7.9 11.8 %collective-permute-start = (bf16[2,256,128]{2,1,0:T(8,128)(2,1)}, bf16[2,256,128]{2,1,0:T(8,128)(2,1)S(1)}, u32[]{:S(2)}, u32[]{:S(2)}) collective-permute-start(bf16[2,256,128]{2,1,0:T(8,128)(2,1)} %param.22), channel_id=1, source_target_pairs={{0,4},{4,8},{8,12},{12,16},{16,20},{20,24},{24,28},{1,5},{5,9},{9,... | collective-permute-start | bytes 393224 | tf_op jit(solution)/shard_map/ppermute | solution.py:14
  15.1 3.0 %copy-start.9 = (bf16[256,896]{1,0:T(8,128)(2,1)S(1)}, bf16[256,896]{1,0:T(8,128)(2,1)}, u32[]{:S(2)}) copy-start(bf16[256,896]{1,0:T(8,128)(2,1)} %param.25) | copy-start | bytes 1376260
  15.3 3.2 %copy-start.15 = (bf16[128,896]{1,0:T(8,128)(2,1)S(1)}, bf16[128,896]{1,0:T(8,128)(2,1)}, u32[]{:S(2)}) copy-start(bf16[128,896]{1,0:T(8,128)(2,1)} %param.19) | copy-start | bytes 688132
  15.3 3.5 %copy-start.16 = (bf16[128,896]{1,0:T(8,128)(2,1)S(1)}, bf16[128,896]{1,0:T(8,128)(2,1)}, u32[]{:S(2)}) copy-start(bf16[128,896]{1,0:T(8,128)(2,1)} %param.24) | copy-start | bytes 688132
  15.3 3.7 %copy-start.17 = (u32[256]{0:T(256)S(1)}, u32[256]{0:T(256)}, u32[]{:S(2)}) copy-start(u32[256]{0:T(256)} %constant.290) | copy-start | bytes 3076
  19.7 3.1 %copy-start.10 = (bf16[2,256,128]{2,1,0:T(8,128)(2,1)}, bf16[2,256,128]{2,1,0:T(8,128)(2,1)S(1)}, u32[]{:S(2)}) copy-start(bf16[2,256,128]{2,1,0:T(8,128)(2,1)S(1)} %collective-permute-done) | copy-start | bytes 393220
  20.1 2.7 %copy-start.2 = (f32[1792,256]{0,1:T(8,128)}, f32[1792,256]{0,1:T(8,128)S(1)}, u32[]{:S(2)}) copy-start(f32[1792,256]{0,1:T(8,128)S(1)} %get-tuple-element.978) | copy-start | bytes 5505028
  68.7 2.7 %copy-start.13 = (bf16[2,256,128]{2,1,0:T(8,128)(2,1)S(1)}, bf16[2,256,128]{2,1,0:T(8,128)(2,1)}, u32[]{:S(2)}) copy-start(bf16[2,256,128]{2,1,0:T(8,128)(2,1)} %param.22) | copy-start | bytes 393220
  71.4 16.8 %copy-start = (bf16[1792,256]{0,1:T(8,128)(2,1)}, bf16[1792,256]{0,1:T(8,128)(2,1)S(1)}, u32[]{:S(2)}) copy-start(bf16[1792,256]{0,1:T(8,128)(2,1)S(1)} %get-tuple-element.972) | copy-start | bytes 2752516
  71.4 1.0 copy-start.11
  86.0 1.2 copy-start.4
  86.0 2.2 copy-start.14
  88.6 1.5 copy-start.12
  91.6 65.6 %collective-permute-start.1 = (bf16[2,256,128]{2,1,0:T(8,128)(2,1)}, bf16[2,256,128]{2,1,0:T(8,128)(2,1)}, u32[]{:S(2)}, u32[]{:S(2)}) collective-permute-start(bf16[2,256,128]{2,1,0:T(8,128)(2,1)} %pad_maximum_fusion.1), channel_id=1, source_target_pairs={{4,0},{8,4},{12,8},{16,12},{20,16},{24,20},{28,24},{5,1},{9,5},{13... | collective-permute-start | bytes 393224 | tf_op jit(solution)/shard_map/ppermute | solution.py:14
  126.1 8.1 %copy-start.3 = (f32[1024,128]{1,0:T(8,128)S(1)}, f32[1024,128]{1,0:T(8,128)}, u32[]{:S(2)}) copy-start(f32[1024,128]{1,0:T(8,128)} %get-tuple-element.778) | copy-start | bytes 1572868
  137.5 13.4 %all-to-all-start = ((bf16[2,8,4,32,128]{4,3,0,1,2:T(8,128)(2,1)}), bf16[2,8,4,32,128]{4,3,0,1,2:T(8,128)(2,1)S(1)}, u32[]{:S(2)}, u32[]{:S(2)}) async-start(bf16[2,8,4,32,128]{4,3,0,1,2:T(8,128)(2,1)} %copy.29), calls=%async_computation | async-start | bytes 1048576 | tf_op jit(solution)/shard_map/all_to_all | solution.py:212
  141.0 105.2 %all-reduce.3.cloned.1.call-start = ((), (), s32[]{:S(2)}) async-start(), calls=%async_computation.2 | async-start | bytes 1048576
  141.8 10.6 %copy-start.1 = (bf16[1792,256]{0,1:T(8,128)(2,1)S(1)}, bf16[1792,256]{0,1:T(8,128)(2,1)}, u32[]{:S(2)}) copy-start(bf16[1792,256]{0,1:T(8,128)(2,1)} %copy-done) | copy-start | bytes 2752516
  151.4 2.7 %copy-start.5 = (bf16[1792,128]{1,0:T(8,128)(2,1)S(1)}, bf16[1792,128]{1,0:T(8,128)(2,1)}, u32[]{:S(2)}) copy-start(bf16[1792,128]{1,0:T(8,128)(2,1)} %get-tuple-element.960) | copy-start | bytes 1376260
  152.4 2.9 %copy-start.7 = (bf16[896,128]{1,0:T(8,128)(2,1)S(1)}, bf16[896,128]{1,0:T(8,128)(2,1)}, u32[]{:S(2)}) copy-start(bf16[896,128]{1,0:T(8,128)(2,1)} %multiply_convert_fusion.2) | copy-start | bytes 688132
  152.4 3.8 %copy-start.6 = (bf16[896,128]{1,0:T(8,128)(2,1)S(1)}, bf16[896,128]{1,0:T(8,128)(2,1)}, u32[]{:S(2)}) copy-start(bf16[896,128]{1,0:T(8,128)(2,1)} %get-tuple-element.962) | copy-start | bytes 688132
  152.5 4.8 %copy-start.8 = (f32[1,256,128]{2,1,0:T(8,128)S(1)}, f32[1,256,128]{2,1,0:T(8,128)}, u32[]{:S(2)}) copy-start(f32[1,256,128]{2,1,0:T(8,128)} %fusion.97) | copy-start | bytes 393220
Sparse Core Ops, SparseCore 0:
  10.6 53.0 all-gather.1
  152.6 93.5 all-reduce.2
where the time goes:
time: 258 us; the launch traced here: 255 us
  waiting for transfers between devices  138 us (53%)
  matrix products  55.5 us (22%)
  local copies, waits for them, and re-layouts  19 us (7%)
  other arithmetic  17.3 us (7%)
  between operations  14.5 us (6%)
  starting transfers between devices  10.2 us (4%)
    unnamed x3, waiting for transfers between devices  88.1 us
    all_gather x1, waiting for transfers between devices, local(): lax.all_gather(prefix_kv, ('group', 'tensor'), axis=1, tiled=True)  40.9 us
    dot_general x7, matrix products, accumulate(): jnp.dot(weights, value_rows, preferred_element_type=jnp.float32)  15.3 us
    dot_general x7, matrix products, backprop(): jnp.einsum('qk,qd->kd', dscore, queries, preferred_element_type=jnp.float32)  11.1 us
    dot_general x7, matrix products, backprop(): jnp.einsum('qk,qd->kd', weights, upstream, preferred_element_type=jnp.flo...  10.4 us
    all_to_all x1, waiting for transfers between devices, local(): lax.all_to_all(arranged.astype(jnp.bfloat16), 'tensor', split_axis=2, con...  9.11 us
    dot_general x12, matrix products, block_scores(): jnp.einsum('qd,kd->qk', queries, key_rows, preferred_element_type=jnp.flo...  8.27 us
    dot_general x7, matrix products, backprop(): jnp.einsum('qd,kd->qk', upstream, value_rows, preferred_element_type=jnp....  6.93 us
  transfers between devices with their start and end apart: 5, of which 3 were waited for; matrix products, arithmetic and copies ran while one was open for 24% of the time, Pallas kernels for 0%

commit v1 on v0

v1 whole, which is shorter than its diff:
```python
import functools
import math

import jax
import jax.numpy as jnp
from jax import lax
from jax.experimental import pallas as pl
from jax.experimental.pallas import tpu as pltpu
from jax.sharding import PartitionSpec as P

D = 128
BF = jnp.bfloat16
F = jnp.float32
SCALE = D**-0.5
SCALE2 = SCALE * math.log2(math.e)
MASKED = -1e30
BACK = 64
NT = (((1,), (1,)), ((), ()))
TN = (((0,), (0,)), ((), ()))
NN = (((1,), (0,)), ((), ()))
BLOCK = 256


def mm(a, b, dims):
    return lax.dot_general(a, b, dims, preferred_element_type=F)


def attend(
    kv_ref, lkv_ref, bias_p_ref, bias_l_ref, qr_ref, gr_ref, qp_ref, gp_ref,
    or_ref, op_ref, dqr_ref, dqp_ref, dkv_ref, dlkv_ref,
    k_s, v_s, s_s, w_s, accp, accl, *, heads,
):
    h = pl.program_id(0)
    keys = k_s.shape[0]
    parts = dkv_ref.shape[0]

    @pl.when(h == 0)
    def _():
        k_s[...] = kv_ref[:, 0].reshape(keys, D)
        v_s[...] = kv_ref[:, 1].reshape(keys, D)
        accp[...] = jnp.zeros_like(accp)
        accl[...] = jnp.zeros_like(accl)

    q = jnp.concatenate([qr_ref[...], qp_ref[...]], 0)
    g = jnp.concatenate([gr_ref[...], gp_ref[...]], 0)
    lk = lkv_ref[0]
    lv = lkv_ref[1]
    blocks = [pl.ds(j, BLOCK) for j in range(0, keys, BLOCK)]
    m = None
    for sl in blocks:
        s = mm(k_s[sl, :], q, NT)
        sr = s[:, :256]
        sp = s[:, 256:] + bias_p_ref[sl, :]
        s_s[sl, :256] = sr
        s_s[sl, 256:] = sp
        mj = jnp.concatenate(
            [jnp.max(sr.reshape(BLOCK // 8, 8, 256), 0), jnp.max(sp.reshape(BLOCK // 8, 8, 128), 0)], 1
        )
        m = mj if m is None else jnp.maximum(m, mj)
    sa = mm(lk[0:192], q[0:128], NT) + bias_l_ref[0]
    sb = mm(lk[128:320], q[128:256], NT) + bias_l_ref[1]
    m = jnp.max(m, 0, keepdims=True)
    ma = jnp.maximum(m[:, :128], jnp.max(sa, 0, keepdims=True))
    mb = jnp.maximum(m[:, 128:256], jnp.max(sb, 0, keepdims=True))
    mc = jnp.concatenate([ma, mb, m[:, 256:]], 1) * SCALE2
    pa = jnp.exp2(sa * SCALE2 - mc[:, :128])
    pb = jnp.exp2(sb * SCALE2 - mc[:, 128:256])
    total = None
    for sl in blocks:
        p = jnp.exp2(s_s[sl, :] * SCALE2 - mc)
        s_s[sl, :] = p
        tj = jnp.sum(p.reshape(BLOCK // 8, 8, 384), 0)
        total = tj if total is None else total + tj
    total = jnp.sum(total, 0, keepdims=True)
    ta = total[:, :128] + jnp.sum(pa, 0, keepdims=True)
    tb = total[:, 128:256] + jnp.sum(pb, 0, keepdims=True)
    inv = 1.0 / jnp.concatenate([ta, tb, total[:, 256:]], 1)
    wa = (pa * inv[:, :128]).astype(BF)
    wb = (pb * inv[:, 128:256]).astype(BF)
    o = jnp.zeros((384, D), F)
    for sl in blocks:
        w = (s_s[sl, :] * inv).astype(BF)
        w_s[sl, :] = w
        o = o + mm(w, v_s[sl, :], TN)
        accp[1, sl, :] += mm(w, g, NN)
    oa = mm(wa, lv[0:192], TN)
    ob = mm(wb, lv[128:320], TN)
    o = jnp.concatenate([o[:128] + oa, o[128:256] + ob, o[256:]], 0).astype(BF)
    or_ref[...] = o[:256]
    op_ref[...] = o[256:]
    delta = jnp.sum((g.astype(F) * o.astype(F)).T, 0, keepdims=True)
    accl[1, 0:192, :] += mm(wa, g[:128], NN)
    accl[1, 128:320, :] += mm(wb, g[128:256], NN)
    dq = jnp.zeros((384, D), F)
    for sl in blocks:
        dp = mm(v_s[sl, :], g, NT)
        ds = (w_s[sl, :].astype(F) * (dp - delta)).astype(BF)
        dq = dq + mm(ds, k_s[sl, :], TN)
        accp[0, sl, :] += mm(ds, q, NN)
    dsa = (wa.astype(F) * (mm(lv[0:192], g[:128], NT) - delta[:, :128])).astype(BF)
    dsb = (wb.astype(F) * (mm(lv[128:320], g[128:256], NT) - delta[:, 128:256])).astype(BF)
    dqa = mm(dsa, lk[0:192], TN)
    dqb = mm(dsb, lk[128:320], TN)
    accl[0, 0:192, :] += mm(dsa, q[:128], NN)
    accl[0, 128:320, :] += mm(dsb, q[128:256], NN)
    dqr_ref[...] = (jnp.concatenate([dq[:128] + dqa, dq[128:256] + dqb], 0) * SCALE).astype(BF)
    dqp_ref[...] = (dq[256:] * SCALE).astype(BF)

    @pl.when(h == heads - 1)
    def _():
        dkv_ref[:, 0] = (accp[0] * SCALE).astype(BF).reshape(parts, keys // parts, D)
        dkv_ref[:, 1] = accp[1].astype(BF).reshape(parts, keys // parts, D)
        dlkv_ref[0] = accl[0] * SCALE
        dlkv_ref[1] = accl[1]


def attention(kv, lkv, bias_p, bias_l, qr, gr, qp, gp):
    heads = qr.shape[1] // D
    keys = kv.shape[0] * kv.shape[2]
    whole = lambda a: pl.BlockSpec(a.shape, lambda h: (0,) * len(a.shape))
    head = lambda n: pl.BlockSpec((n, D), lambda h: (0, h))
    shape = jax.ShapeDtypeStruct
    outs = [shape(qr.shape, BF), shape(qp.shape, BF), shape(qr.shape, BF), shape(qp.shape, BF)]
    outs += [shape(kv.shape, BF), shape(lkv.shape, F)]
    pairs = keys * 384 * heads
    return pl.pallas_call(
        functools.partial(attend, heads=heads),
        grid=(heads,),
        in_specs=[whole(kv), whole(lkv), whole(bias_p), whole(bias_l), head(256), head(256), head(128), head(128)],
        out_specs=[head(256), head(128), head(256), head(128), whole(outs[4]), whole(outs[5])],
        out_shape=outs,
        scratch_shapes=[
            pltpu.VMEM((keys, D), BF),
            pltpu.VMEM((keys, D), BF),
            pltpu.VMEM((keys, 384), F),
            pltpu.VMEM((keys, 384), BF),
            pltpu.VMEM((2, keys, D), F),
            pltpu.VMEM((2, 320, D), F),
        ],
        compiler_params=pltpu.CompilerParams(vmem_limit_bytes=48 * 2**20),
        cost_estimate=pl.CostEstimate(flops=pairs * 1280, bytes_accessed=4 * 2**20, transcendentals=pairs),
        name="attend",
    )(kv, lkv, bias_p, bias_l, qr, gr, qp, gp)


def local(prompt_q, prefix_kv, resp_q, resp_kv, resp_segs, grad_prompt_out, grad_resp_out):
    groups = lax.axis_size("group")
    tensors = lax.axis_size("tensor")
    group_rank = lax.axis_index("group")
    rows = prefix_kv.shape[1]
    resp_dev = resp_q.shape[0]
    prompt_dev = prompt_q.shape[0]
    keys = rows * groups * tensors
    both = ("group", "tensor")

    by_head = prefix_kv.reshape(2, rows, tensors, D).transpose(2, 0, 1, 3)
    to_send = jnp.broadcast_to(by_head[None], (groups,) + by_head.shape).reshape(-1, 2, rows, D)
    kv = lax.all_to_all(to_send, both, 0, 0, tiled=True)
    prior = lax.ppermute(
        resp_kv[:, resp_dev - BACK :], "group", [(i, i + 1) for i in range(groups - 1)]
    )
    lkv = jnp.concatenate([prior, resp_kv], 1)

    segs = jnp.concatenate([jnp.full((BACK,), -1, jnp.int32), resp_segs])
    segs = lax.dynamic_slice_in_dim(segs, group_rank * resp_dev, BACK + resp_dev)
    places = jnp.arange(BACK + resp_dev, dtype=jnp.int32)

    def local_bias(k0, k1, q0, q1):
        same = segs[k0:k1, None] == segs[None, q0:q1]
        return jnp.where(same & (places[k0:k1, None] <= places[None, q0:q1]), 0.0, MASKED).astype(F)

    bias_l = jnp.stack([local_bias(0, 192, 64, 192), local_bias(128, 320, 192, 320)])
    query_rows = group_rank * prompt_dev + jnp.arange(prompt_dev, dtype=jnp.int32)
    bias_p = jnp.where(
        jnp.arange(keys, dtype=jnp.int32)[:, None] <= query_rows[None, :], 0.0, MASKED
    ).astype(F)

    resp_out, prompt_out, grad_resp_q, grad_prompt_q, terms, local_terms = attention(
        kv, lkv, bias_p, bias_l, resp_q, grad_resp_out, prompt_q, grad_prompt_out
    )
    arrived = lax.all_to_all(terms, both, 0, 0, tiled=True)
    later = lax.ppermute(
        local_terms[:, :BACK].astype(BF), "group", [(i, i - 1) for i in range(1, groups)]
    )
    grad_resp_kv = jnp.concatenate(
        [local_terms[:, BACK:resp_dev], local_terms[:, resp_dev:] + later.astype(F)], 1
    ).astype(BF)
    summed = arrived.reshape(groups, tensors, 2, rows, D).astype(F).sum(0).astype(BF)
    grad_prefix_kv = summed.transpose(1, 2, 0, 3).reshape(2, rows, tensors * D)
    return (prompt_out, resp_out, grad_prompt_q, grad_resp_q, grad_prefix_kv, grad_resp_kv)


def solution(mesh):
    wide = P(("prompt", "group"), "tensor")
    cache = P(None, ("prompt", "group", "tensor"), None)
    packed = P(None, ("prompt", "group"), "tensor")
    return jax.shard_map(
        local,
        mesh=mesh,
        in_specs=(wide, cache, wide, packed, P("prompt"), wide, wide),
        out_specs=(wide, wide, wide, wide, cache, packed),
        check_vma=False,
    )
```

time: 258 us -> 62.9 us (0.24)
  waiting for transfers between devices: 138 us -> 15.7 us
  matrix products: 55.5 us -> 0 us
  Pallas kernels: 0 us -> 21 us
  other arithmetic: 17.3 us -> 1.03 us
  between operations: 14.5 us -> 0.85 us
  local copies, waits for them, and re-layouts: 19 us -> 5.48 us
  starting transfers between devices: 10.2 us -> 18.3 us
    unnamed x3 -> x0, waiting for transfers between devices: 88.1 us -> none
    dot_general x47 -> x0, matrix products: 55.5 us -> none  [the longest x7 15.3 us: accumulate(): jnp.dot(weights, value_rows, preferred_element_type=jnp.float32)]
    all_gather x1 -> x0, waiting for transfers between devices: 40.9 us -> none  [local(): lax.all_gather(prefix_kv, ('group', 'tensor'), axis=1, tiled=True)]
    pallas_call x0 -> x1, Pallas kernels: none -> 21 us  [attention(): pl.pallas_call(functools.partial(attend, heads=heads), grid=(heads,), in_...]
    all_to_all x1 -> x2, starting transfers between devices: 3.47 us -> 11.6 us  [the longest x1 7.04 us: local(): kv = lax.all_to_all(to_send, both, 0, 0, tiled=True)]
    ppermute x2, waiting for transfers between devices: 0.01 us -> 6.42 us  [the longest x1 6.42 us: local(): lax.ppermute(local_terms[:, :BACK].astype(BF), 'group', [(i, i - 1) for i...]
    reshape x8 -> x2, local copies, waits for them, and re-layouts: 6.75 us -> 0.66 us  [the longest x1 0.64 us: local(): grad_prefix_kv = summed.transpose(1, 2, 0, 3).reshape(2, rows, tensors * D)]
    reduce_sum x8 -> x1, other arithmetic: 5.68 us -> 0.08 us  [local(): arrived.reshape(groups, tensors, 2, rows, D).astype(F).sum(0).astype(BF)]
  transfers between devices with their start and end apart: 5 -> 4, of which waited for: 3 -> 3; matrix products, arithmetic and copies ran while one was open for 24% -> 4% of each run, Pallas kernels for 0% -> 0%
where the time goes in v1:
time: 62.9 us; the launch traced here: 62.4 us
  Pallas kernels  21 us (33%)
  starting transfers between devices  18.3 us (29%)
  waiting for transfers between devices  15.7 us (25%)
  local copies, waits for them, and re-layouts  5.48 us (9%)
  other arithmetic  1.03 us (2%)
  between operations  0.85 us (1%)
    pallas_call x1, Pallas kernels, attention(): pl.pallas_call(functools.partial(attend, heads=heads), grid=(heads,), in_...  21 us
    all_to_all x1, waiting for transfers between devices, local(): kv = lax.all_to_all(to_send, both, 0, 0, tiled=True)  8.49 us
    all_to_all x1, starting transfers between devices, local(): kv = lax.all_to_all(to_send, both, 0, 0, tiled=True)  7.04 us
    ppermute x1, waiting for transfers between devices, local(): lax.ppermute(local_terms[:, :BACK].astype(BF), 'group', [(i, i - 1) for i...  6.42 us
    all_to_all x1, starting transfers between devices, local(): arrived = lax.all_to_all(terms, both, 0, 0, tiled=True)  4.55 us
    ppermute x1, starting transfers between devices, local(): lax.ppermute(resp_kv[:, resp_dev - BACK:], 'group', [(i, i + 1) for i in...  4.5 us
    ppermute x1, starting transfers between devices, local(): lax.ppermute(local_terms[:, :BACK].astype(BF), 'group', [(i, i - 1) for i...  2.24 us
  transfers between devices with their start and end apart: 4, of which 3 were waited for; matrix products, arithmetic and copies ran while one was open for 4% of the time, Pallas kernels for 0%

profile of v1, /device:TPU:1, one launch (start us, length us, event | category | flops | bytes accessed | tf_op | source)
XLA Modules:
  0.0 62.4 jit_solution(11801316132111985516)
XLA Ops:
  0.6 0.0 copy-start.6
  0.6 0.8 %slice.38 = bf16[2,64,128]{2,1,0:T(8,128)(2,1)S(1)} slice(bf16[2,256,128]{2,1,0:T(8,128)(2,1)} %param.10), slice={[0:2], [192:256], [0:128]} | slice | bytes 65536 | tf_op jit(solution)/shard_map/slice | solution.py:160
  1.4 4.5 %collective-permute-start = (bf16[2,64,128]{2,1,0:T(8,128)(2,1)S(1)}, bf16[2,64,128]{2,1,0:T(8,128)(2,1)S(1)}, u32[]{:S(2)}, u32[]{:S(2)}) collective-permute-start(bf16[2,64,128]{2,1,0:T(8,128)(2,1)S(1)} %slice.38), channel_id=1, source_target_pairs={{0,4},{4,8},{8,12},{12,16},{16,20},{20,24},{24,28},{1,5},{5,9},{9,... | collective-permute-start | bytes 98312 | tf_op jit(solution)/shard_map/ppermute | solution.py:159
  5.9 0.0 copy-done.6
  6.0 0.9 %broadcast_in_dim.18 = bf16[8,4,2,32,128]{4,3,2,1,0:T(8,128)(2,1)} broadcast(bf16[4,2,32,128]{3,2,1,0:T(8,128)(2,1)S(1)} %copy.15), dimensions={1,2,3,4} | broadcast | bytes 589824 | tf_op jit(solution)/shard_map/broadcast_in_dim | solution.py:157
  6.9 0.0 copy-start.5
  6.9 7.0 %all-to-all-start = ((bf16[32,2,32,128]{3,2,1,0:T(8,128)(2,1)}), bf16[32,2,32,128]{3,2,1,0:T(8,128)(2,1)S(1)}, u32[]{:S(2)}, u32[]{:S(2)}) async-start(bf16[32,2,32,128]{3,2,1,0:T(8,128)(2,1)} %bitcast.1), calls=%async_computation | async-start | bytes 1048576 | tf_op jit(solution)/shard_map/all_to_all | solution.py:158
  14.0 0.0 copy-start.7
  14.0 0.7 %copy-done.7 = s32[2048]{0:T(1024)S(1)} copy-done((s32[2048]{0:T(1024)S(1)}, s32[2048]{0:T(1024)}, u32[]{:S(2)}) %copy-start.7) | copy-done | bytes 8216
  14.7 0.1 pad_dynamic-slice_fusion
  14.7 0.1 fusion.2
  14.8 0.1 slice.46
  14.9 0.0 copy-start.8
  14.9 0.1 slice.42
  15.0 0.5 copy-done.8
  15.5 0.0 slice-start.1
  15.5 0.7 %slice-done.1 = s32[192]{0:T(256)S(1)} async-done(((s32[320]{0:T(512)}), s32[192]{0:T(256)S(1)}, s32[]{:S(2)}) %slice-start.1) | async-done | bytes 792 | tf_op jit(solution)/shard_map/slice | solution.py:170
  16.2 0.0 copy-start.3
  16.2 0.2 and_select_fusion
  16.3 0.0 copy-start.1
  16.4 0.1 fusion.bias_p_ref
  16.4 0.0 copy-start
  16.5 0.0 copy-start.2
  16.5 0.0 collective-permute-done
  16.5 0.0 copy-done.5
  16.5 8.5 %all-to-all-done.kv_ref = bf16[32,2,32,128]{3,2,1,0:T(8,128)(2,1)S(1)} async-done(((bf16[32,2,32,128]{3,2,1,0:T(8,128)(2,1)}), bf16[32,2,32,128]{3,2,1,0:T(8,128)(2,1)S(1)}, u32[]{:S(2)}, u32[]{:S(2)}) %all-to-all-start) | async-done | bytes 524320 | tf_op jit(solution)/shard_map/all_to_all | solution.py:158
  25.0 0.0 copy-done.3
  25.0 0.0 copy-done.1
  25.0 0.0 copy-done
  25.0 0.0 copy-done.2
  25.0 21.0 %attend.1 = (bf16[256,896]{1,0:T(8,128)(2,1)}, bf16[128,896]{1,0:T(8,128)(2,1)}, bf16[256,896]{1,0:T(8,128)(2,1)}, bf16[128,896]{1,0:T(8,128)(2,1)}, bf16[32,2,3...) custom-call(bf16[32,2,32,128]{3,2,1,0:T(8,128)(2,1)S(1)} %all-to-all-done.kv_ref, ...), custom_call_target="tpu_custom_call" | custom-call | flops 3523215360 | bytes 4194304 | tf_op jit(solution)/shard_map/attend/pallas_call | solution.py:126
  46.0 4.5 %all-to-all-start.1 = ((bf16[32,2,32,128]{3,2,1,0:T(8,128)(2,1)}), bf16[32,2,32,128]{3,2,1,0:T(8,128)(2,1)S(1)}, u32[]{:S(2)}, u32[]{:S(2)}) async-start(bf16[32,2,32,128]{3,2,1,0:T(8,128)(2,1)} %get-tuple-element.16), calls=%async_computation.1 | async-start | bytes 1048576 | tf_op jit(solution)/shard_map/all_to_all | solution.py:181
  50.6 0.0 copy-start.4
  50.6 2.2 %collective-permute-start.1 = (bf16[2,64,128]{2,1,0:T(8,128)(2,1)S(1)}, bf16[2,64,128]{2,1,0:T(8,128)(2,1)S(1)}, u32[]{:S(2)}, u32[]{:S(2)}) collective-permute-start(bf16[2,64,128]{2,1,0:T(8,128)(2,1)S(1)} %slice.51), channel_id=1, source_target_pairs={{4,0},{8,4},{12,8},{16,12},{20,16},{24,20},{28,24},{5,1},{9,5},{13... | collective-permute-start | bytes 98312 | tf_op jit(solution)/shard_map/ppermute | solution.py:182
  52.9 0.0 copy-done.4
  52.9 6.4 %collective-permute-done.1 = bf16[2,64,128]{2,1,0:T(8,128)(2,1)S(1)} collective-permute-done((bf16[2,64,128]{2,1,0:T(8,128)(2,1)S(1)}, bf16[2,64,128]{2,1,0:T(8,128)(2,1)S(1)}, u32[]{:S(2)}, u32[]{:S(2)}) %collective-permute-start.1) | collective-permute-done | bytes 32800 | tf_op jit(solution)/shard_map/ppermute | solution.py:182
  59.3 0.0 slice-start
  59.3 0.9 %slice-done = bf16[2,192,128]{2,1,0:T(8,128)(2,1)S(1)} async-done(((bf16[2,320,128]{2,1,0:T(8,128)(2,1)}), bf16[2,192,128]{2,1,0:T(8,128)(2,1)S(1)}, s32[]{:S(2)}) %slice-start) | async-done | bytes 98328 | tf_op jit(solution)/shard_map/slice | solution.py:186
  60.2 0.7 %pad_maximum_fusion.2 = bf16[2,256,128]{2,1,0:T(8,128)(2,1)} fusion(bf16[2,64,128]{2,1,0:T(8,128)(2,1)S(1)} %add_convert_fusion, bf16[2,192,128]{2,1,0:T(8,128)(2,1)S(1)} %slice-done), kind=kLoop, calls=%fused_computation.4 | loop fusion | flops 262144 | bytes 262144 | tf_op jit(solution)/shard_map/concatenate | solution.py:185
  60.9 0.8 %all-to-all-done.1 = bf16[32,2,32,128]{3,2,1,0:T(8,128)(2,1)S(1)} async-done(((bf16[32,2,32,128]{3,2,1,0:T(8,128)(2,1)}), bf16[32,2,32,128]{3,2,1,0:T(8,128)(2,1)S(1)}, u32[]{:S(2)}, u32[]{:S(2)}) %all-to-all-start.1) | async-done | bytes 524320 | tf_op jit(solution)/shard_map/all_to_all | solution.py:181
  61.7 0.1 reduce_sum.12
  61.8 0.6 %copy_bitcast_fusion = bf16[2,32,512]{2,1,0:T(8,128)(2,1)} fusion(bf16[4,2,32,128]{3,2,1,0:T(8,128)(2,1)S(1)} %reduce_sum.12), kind=kLoop, calls=%fused_computation.7 | loop fusion | bytes 131072 | tf_op jit(solution)/shard_map/reshape | solution.py:189
  (12 shorter events, 0.1 us)
Async XLA Ops:
  0.6 5.3 %copy-start.6 = (bf16[2,32,512]{2,1,0:T(8,128)(2,1)S(1)}, bf16[2,32,512]{2,1,0:T(8,128)(2,1)}, u32[]{:S(2)}) copy-start(bf16[2,32,512]{2,1,0:T(8,128)(2,1)} %param.8) | copy-start | bytes 196612
  1.4 15.0 %collective-permute-start = (bf16[2,64,128]{2,1,0:T(8,128)(2,1)S(1)}, bf16[2,64,128]{2,1,0:T(8,128)(2,1)S(1)}, u32[]{:S(2)}, u32[]{:S(2)}) collective-permute-start(bf16[2,64,128]{2,1,0:T(8,128)(2,1)S(1)} %slice.38), channel_id=1, source_target_pairs={{0,4},{4,8},{8,12},{12,16},{16,20},{20,24},{24,28},{1,5},{5,9},{9,... | collective-permute-start | bytes 98312 | tf_op jit(solution)/shard_map/ppermute | solution.py:159
  6.9 9.6 %copy-start.5 = (bf16[2,256,128]{2,1,0:T(8,128)(2,1)S(1)}, bf16[2,256,128]{2,1,0:T(8,128)(2,1)}, u32[]{:S(2)}) copy-start(bf16[2,256,128]{2,1,0:T(8,128)(2,1)} %param.10) | copy-start | bytes 393220
  6.9 18.1 %all-to-all-start = ((bf16[32,2,32,128]{3,2,1,0:T(8,128)(2,1)}), bf16[32,2,32,128]{3,2,1,0:T(8,128)(2,1)S(1)}, u32[]{:S(2)}, u32[]{:S(2)}) async-start(bf16[32,2,32,128]{3,2,1,0:T(8,128)(2,1)} %bitcast.1), calls=%async_computation | async-start | bytes 1048576 | tf_op jit(solution)/shard_map/all_to_all | solution.py:158
  14.0 0.7 %copy-start.7 = (s32[2048]{0:T(1024)S(1)}, s32[2048]{0:T(1024)}, u32[]{:S(2)}) copy-start(s32[2048]{0:T(1024)} %param.11) | copy-start | bytes 24580
  14.9 0.6 copy-start.8
  15.5 0.7 %slice-start.1 = ((s32[320]{0:T(512)}), s32[192]{0:T(256)S(1)}, s32[]{:S(2)}) async-start(s32[320]{0:T(512)} %copy-done.8), calls=%async_computation.3 | async-start | bytes 2048 | tf_op jit(solution)/shard_map/slice | solution.py:170
  16.2 8.8 %copy-start.3 = (bf16[128,896]{1,0:T(8,128)(2,1)S(1)}, bf16[128,896]{1,0:T(8,128)(2,1)}, u32[]{:S(2)}) copy-start(bf16[128,896]{1,0:T(8,128)(2,1)} %gp_ref.1) | copy-start | bytes 688132
  16.3 8.7 %copy-start.1 = (bf16[256,896]{1,0:T(8,128)(2,1)S(1)}, bf16[256,896]{1,0:T(8,128)(2,1)}, u32[]{:S(2)}) copy-start(bf16[256,896]{1,0:T(8,128)(2,1)} %gr_ref.1) | copy-start | bytes 1376260
  16.4 8.6 %copy-start = (bf16[256,896]{1,0:T(8,128)(2,1)S(1)}, bf16[256,896]{1,0:T(8,128)(2,1)}, u32[]{:S(2)}) copy-start(bf16[256,896]{1,0:T(8,128)(2,1)} %qr_ref.1) | copy-start | bytes 1376260
  16.5 8.6 %copy-start.2 = (bf16[128,896]{1,0:T(8,128)(2,1)S(1)}, bf16[128,896]{1,0:T(8,128)(2,1)}, u32[]{:S(2)}) copy-start(bf16[128,896]{1,0:T(8,128)(2,1)} %qp_ref.1) | copy-start | bytes 688132
  46.0 15.7 %all-to-all-start.1 = ((bf16[32,2,32,128]{3,2,1,0:T(8,128)(2,1)}), bf16[32,2,32,128]{3,2,1,0:T(8,128)(2,1)S(1)}, u32[]{:S(2)}, u32[]{:S(2)}) async-start(bf16[32,2,32,128]{3,2,1,0:T(8,128)(2,1)} %get-tuple-element.16), calls=%async_computation.1 | async-start | bytes 1048576 | tf_op jit(solution)/shard_map/all_to_all | solution.py:181
  50.6 2.3 %copy-start.4 = (bf16[2,320,128]{2,1,0:T(8,128)(2,1)}, bf16[2,320,128]{2,1,0:T(8,128)(2,1)S(1)}, u32[]{:S(2)}) copy-start(bf16[2,320,128]{2,1,0:T(8,128)(2,1)S(1)} %convert.9) | copy-start | bytes 491524
  50.6 8.7 %collective-permute-start.1 = (bf16[2,64,128]{2,1,0:T(8,128)(2,1)S(1)}, bf16[2,64,128]{2,1,0:T(8,128)(2,1)S(1)}, u32[]{:S(2)}, u32[]{:S(2)}) collective-permute-start(bf16[2,64,128]{2,1,0:T(8,128)(2,1)S(1)} %slice.51), channel_id=1, source_target_pairs={{4,0},{8,4},{12,8},{16,12},{20,16},{24,20},{28,24},{5,1},{9,5},{13... | collective-permute-start | bytes 98312 | tf_op jit(solution)/shard_map/ppermute | solution.py:182
  59.3 0.9 %slice-start = ((bf16[2,320,128]{2,1,0:T(8,128)(2,1)}), bf16[2,192,128]{2,1,0:T(8,128)(2,1)S(1)}, s32[]{:S(2)}) async-start(bf16[2,320,128]{2,1,0:T(8,128)(2,1)} %copy-done.4), calls=%async_computation.2 | async-start | bytes 196608 | tf_op jit(solution)/shard_map/slice | solution.py:186

commit v2 on v1

v2 whole, which is shorter than its diff:
```python
import math

import jax
import jax.numpy as jnp
from jax import lax
from jax.experimental import pallas as pl
from jax.experimental.pallas import tpu as pltpu
from jax.sharding import PartitionSpec as P

D = 128
BF = jnp.bfloat16
F = jnp.float32
SCALE = D**-0.5
SCALE2 = SCALE * math.log2(math.e)
MASKED = -1e30
BACK = 64
NT = (((1,), (1,)), ((), ()))
TN = (((0,), (0,)), ((), ()))
NN = (((1,), (0,)), ((), ()))
CHUNK = 512


def mm(a, b, dims):
    return lax.dot_general(a, b, dims, preferred_element_type=F)


def fold(x, op):
    return op(x.reshape(x.shape[0] // 8, 8, x.shape[1]), 0)


def stack_heads(ref, rows):
    return jnp.concatenate([ref[rows, i : i + D] for i in range(0, ref.shape[1], D)], 0)


def halves(resp):
    half = resp // 2
    return [(i, slice(i * half, (i + 1) * half), slice(i * half, i * half + half + BACK)) for i in range(2)]


def local_forward(lkv_ref, bias_ref, q_ref, g_ref, p_ref, stat_ref):
    heads = q_ref.shape[1] // D
    for i, rows, keys in halves(q_ref.shape[0]):
        q = stack_heads(q_ref, rows)
        g = stack_heads(g_ref, rows)
        s = mm(lkv_ref[0, keys], q, NT) + jnp.concatenate([bias_ref[i]] * heads, 1)
        m = jnp.max(s, 0, keepdims=True)
        p = jnp.exp2((s - m) * SCALE2)
        dp = mm(lkv_ref[1, keys], g, NT)
        p_ref[i] = p.astype(BF)
        total = jnp.sum(p, 0, keepdims=True)
        mix = jnp.sum(p * dp, 0, keepdims=True)
        for h in range(heads):
            c = slice(h * 128, (h + 1) * 128)
            stat_ref[h, 0:1, rows] = m[:, c]
            stat_ref[h, 1:2, rows] = total[:, c]
            stat_ref[h, 2:3, rows] = mix[:, c]


def local_backward(lkv_ref, p_ref, fs_ref, q_ref, g_ref, o1_ref, dq1_ref, dlkv_ref, o_ref, dq_ref):
    heads = q_ref.shape[1] // D
    terms = []
    for i, rows, keys in halves(q_ref.shape[0]):
        q = stack_heads(q_ref, rows)
        g = stack_heads(g_ref, rows)
        f = jnp.concatenate([fs_ref[h, 0:1, rows] for h in range(heads)], 1)
        delta = jnp.concatenate([fs_ref[h, 1:2, rows] for h in range(heads)], 1)
        k = lkv_ref[0, keys]
        v = lkv_ref[1, keys]
        wf = p_ref[i].astype(F) * f
        w = wf.astype(BF)
        ds = (wf * (mm(v, g, NT) - delta)).astype(BF)
        terms.append((mm(ds, q, NN) * SCALE, mm(w, g, NN)))
        o = mm(w, v, TN)
        dq = mm(ds, k, TN) * SCALE
        for h in range(heads):
            c = slice(h * D, (h + 1) * D)
            r = slice(h * 128, (h + 1) * 128)
            o_ref[rows, c] = (o[r] + o1_ref[rows, c]).astype(BF)
            dq_ref[rows, c] = (dq[r] + dq1_ref[rows, c]).astype(BF)
    for x in range(2):
        a, b = terms[0][x], terms[1][x]
        dlkv_ref[x, 0:128] = a[0:128]
        dlkv_ref[x, 128:192] = a[128:192] + b[0:64]
        dlkv_ref[x, 192:320] = b[64:192]


def prefix_attention(
    first_ref, kv_ref, stat_ref, qr_ref, gr_ref, qp_ref, gp_ref,
    or_ref, op_ref, dqr_ref, dqp_ref, fs_ref, dkv_ref,
    k_s, v_s, kt_s, vt_s, s_s, d_s, acck, accv,
):
    heads = qr_ref.shape[1] // D
    resp = qr_ref.shape[0]
    keys = k_s.shape[0]
    parts = dkv_ref.shape[0]
    slots = s_s.shape[0]
    k_s[...] = kv_ref[:, 0].reshape(keys, D)
    v_s[...] = kv_ref[:, 1].reshape(keys, D)
    kt_s[...] = k_s[...].T
    vt_s[...] = v_s[...].T
    first = first_ref[0]
    ahead = lax.broadcasted_iota(jnp.int32, (CHUNK, 128), 0) - lax.broadcasted_iota(
        jnp.int32, (CHUNK, 128), 1
    )
    held = {}

    def load(a, b, h):
        c = slice(h * D, (h + 1) * D)
        return jnp.concatenate([a[:, c], b[:, c]], 0)

    def scores(h, k0):
        if k0 == 0:
            held[h] = {"q": load(qr_ref, qp_ref, h), "g": load(gr_ref, gp_ref, h)}
        d = held[h]
        at = slice(k0, k0 + CHUNK)
        s = mm(k_s[at, :], d["q"], NT)
        s = jnp.concatenate([s[:, :resp], jnp.where(ahead <= first - k0, s[:, resp:], MASKED)], 1)
        s_s[h % slots, at, :] = s
        peak = fold(s, jnp.max)
        d["m"] = jnp.maximum(d["m"], peak) if k0 else peak
        d_s[h % slots, at, :] = mm(v_s[at, :], d["g"], NT)

    def raised(h, k0):
        d = held[h]
        if k0 == 0:
            m = jnp.max(d["m"], 0, keepdims=True)
            peak = stat_ref[h, 0:1]
            both = jnp.maximum(m[:, :resp], peak)
            d["f"] = jnp.exp2((peak - both) * SCALE2)
            d["m"] = jnp.concatenate([both, m[:, resp:]], 1) * SCALE2
        at = slice(k0, k0 + CHUNK)
        p = jnp.exp2(s_s[h % slots, at, :] * SCALE2 - d["m"])
        s_s[h % slots, at, :] = p
        total = fold(p, jnp.sum)
        mix = fold(p * d_s[h % slots, at, :], jnp.sum)
        d["l"] = d["l"] + total if k0 else total
        d["t"] = d["t"] + mix if k0 else mix

    def products(h, k0):
        d = held[h]
        if k0 == 0:
            f = d["f"]
            l = jnp.sum(d["l"], 0, keepdims=True)
            t = jnp.sum(d["t"], 0, keepdims=True)
            l = jnp.concatenate([l[:, :resp] + f * stat_ref[h, 1:2], l[:, resp:]], 1)
            t = jnp.concatenate([t[:, :resp] + f * stat_ref[h, 2:3], t[:, resp:]], 1)
            d["inv"] = 1.0 / l
            d["delta"] = t * d["inv"]
            fs_ref[h, 0:1] = f * d["inv"][:, :resp]
            fs_ref[h, 1:2] = d["delta"][:, :resp]
        at = slice(k0, k0 + CHUNK)
        w = s_s[h % slots, at, :] * d["inv"]
        ds = (w * (d_s[h % slots, at, :] - d["delta"])).astype(BF)
        w = w.astype(BF)
        o = mm(vt_s[:, at], w, NN)
        dq = mm(kt_s[:, at], ds, NN)
        d["o"] = d["o"] + o if k0 else o
        d["dq"] = d["dq"] + dq if k0 else dq
        dv = mm(w, d["g"], NN)
        dk = mm(ds, d["q"], NN)
        accv[at, :] = accv[at, :] + dv if h else dv
        acck[at, :] = acck[at, :] + dk if h else dk
        if k0 + CHUNK == keys:
            c = slice(h * D, (h + 1) * D)
            o = d["o"].T
            dq = d["dq"].T * SCALE
            or_ref[:, c] = o[:resp]
            op_ref[:, c] = o[resp:].astype(BF)
            dqr_ref[:, c] = dq[:resp]
            dqp_ref[:, c] = dq[resp:].astype(BF)
            del held[h]

    for i in range(heads + 2):
        for k0 in range(0, keys, CHUNK):
            for late, stage in enumerate((scores, raised, products)):
                if 0 <= i - late < heads:
                    stage(i - late, k0)
    dkv_ref[:, 0] = (acck[...] * SCALE).astype(BF).reshape(parts, keys // parts, D)
    dkv_ref[:, 1] = accv[...].astype(BF).reshape(parts, keys // parts, D)


def shape(*dims, dtype=BF):
    return jax.ShapeDtypeStruct(dims, dtype)


def call(body, outs, operands, flops, scratch=(), scalars=0):
    vmem = pl.BlockSpec(memory_space=pltpu.VMEM)
    return pl.pallas_call(
        body,
        in_specs=[pl.BlockSpec(memory_space=pltpu.SMEM)] * scalars + [vmem] * (len(operands) - scalars),
        out_specs=[vmem] * len(outs),
        out_shape=outs,
        scratch_shapes=scratch,
        compiler_params=pltpu.CompilerParams(vmem_limit_bytes=48 * 2**20),
        cost_estimate=pl.CostEstimate(flops=flops, bytes_accessed=4 * 2**20, transcendentals=0),
        name=body.__name__,
    )(*operands)


def local(prompt_q, prefix_kv, resp_q, resp_kv, resp_segs, grad_prompt_out, grad_resp_out):
    groups = lax.axis_size("group")
    tensors = lax.axis_size("tensor")
    group_rank = lax.axis_index("group")
    rows = prefix_kv.shape[1]
    resp_dev = resp_q.shape[0]
    prompt_dev = prompt_q.shape[0]
    keys = rows * groups * tensors
    both = ("group", "tensor")

    by_head = prefix_kv.reshape(2, rows, tensors, D).transpose(2, 0, 1, 3)
    to_send = jnp.broadcast_to(by_head[None], (groups,) + by_head.shape).reshape(-1, 2, rows, D)
    kv = lax.all_to_all(to_send, both, 0, 0, tiled=True)
    prior = lax.ppermute(
        resp_kv[:, resp_dev - BACK :], "group", [(i, i + 1) for i in range(groups - 1)]
    )
    lkv = jnp.concatenate([prior, resp_kv], 1)

    segs = jnp.concatenate([jnp.full((BACK,), -1, jnp.int32), resp_segs])
    segs = lax.dynamic_slice_in_dim(segs, group_rank * resp_dev, BACK + resp_dev)
    places = jnp.arange(BACK + resp_dev, dtype=jnp.int32)

    def local_bias(k0, k1, q0, q1):
        same = segs[k0:k1, None] == segs[None, q0:q1]
        return jnp.where(same & (places[k0:k1, None] <= places[None, q0:q1]), 0.0, MASKED).astype(F)

    bias_l = jnp.stack([local_bias(0, 192, 64, 192), local_bias(128, 320, 192, 320)])
    first = (group_rank * prompt_dev).astype(jnp.int32).reshape(1)
    width = resp_q.shape[1]
    heads = width // D
    rows_all = resp_dev + prompt_dev
    work = 2 * D * heads
    p_loc, stats = call(
        local_forward,
        [shape(2, 192, heads * 128), shape(heads, 8, resp_dev, dtype=F)],
        (lkv, bias_l, resp_q, grad_resp_out),
        work * 2 * 192 * resp_dev,
    )

    wide = (resp_dev, width)
    vm = pltpu.VMEM
    out1, prompt_out, dq1, grad_prompt_q, factors, terms = call(
        prefix_attention,
        [
            shape(*wide, dtype=F), shape(prompt_dev, width), shape(*wide, dtype=F), shape(prompt_dev, width),
            shape(heads, 8, resp_dev, dtype=F), shape(*kv.shape),
        ],
        (first, kv, stats, resp_q, grad_resp_out, prompt_q, grad_prompt_out),
        work * 6 * keys * rows_all,
        [vm((keys, D), BF), vm((keys, D), BF), vm((D, keys), BF), vm((D, keys), BF)]
        + [vm((3, keys, rows_all), F)] * 2
        + [vm((keys, D), F)] * 2,
        1,
    )
    arrived = lax.all_to_all(terms, both, 0, 0, tiled=True)
    local_terms, resp_out, grad_resp_q = call(
        local_backward,
        [shape(2, BACK + resp_dev, D, dtype=F), shape(*wide), shape(*wide)],
        (lkv, p_loc, factors, resp_q, grad_resp_out, out1, dq1),
        work * 5 * 192 * resp_dev,
    )
    later = lax.ppermute(
        local_terms[:, :BACK].astype(BF), "group", [(i, i - 1) for i in range(1, groups)]
    )
    grad_resp_kv = jnp.concatenate(
        [local_terms[:, BACK:resp_dev], local_terms[:, resp_dev:] + later.astype(F)], 1
    ).astype(BF)
    summed = arrived.reshape(groups, tensors, 2, rows, D).astype(F).sum(0).astype(BF)
    grad_prefix_kv = summed.transpose(1, 2, 0, 3).reshape(2, rows, tensors * D)
    return (prompt_out, resp_out, grad_prompt_q, grad_resp_q, grad_prefix_kv, grad_resp_kv)


def solution(mesh):
    wide = P(("prompt", "group"), "tensor")
    cache = P(None, ("prompt", "group", "tensor"), None)
    packed = P(None, ("prompt", "group"), "tensor")
    return jax.shard_map(
        local,
        mesh=mesh,
        in_specs=(wide, cache, wide, packed, P("prompt"), wide, wide),
        out_specs=(wide, wide, wide, wide, cache, packed),
        check_vma=False,
    )
```

time: 62.9 us -> 56.9 us (0.905)
  Pallas kernels: 21 us -> 15 us
  waiting for transfers between devices: 15.7 us -> 10.1 us
  local copies, waits for them, and re-layouts: 5.48 us -> 11 us
    pallas_call x1 -> x3, Pallas kernels: 21 us -> 15 us  [call(): pl.pallas_call(body, in_specs=[pl.BlockSpec(memory_space=pltpu.SMEM)] * s...]
    unnamed x18 -> x25, local copies, waits for them, and re-layouts: 1.23 us -> 6.73 us
    ppermute x1, waiting for transfers between devices: 6.42 us -> 3.28 us  [local(): lax.ppermute(local_terms[:, :BACK].astype(BF), 'group', [(i, i - 1) for i...]
    all_to_all x1, waiting for transfers between devices: 8.49 us -> 6.19 us  [local(): kv = lax.all_to_all(to_send, both, 0, 0, tiled=True)]
  transfers between devices with their start and end apart: 4 -> 4, of which waited for: 3 -> 3; matrix products, arithmetic and copies ran while one was open for 4% -> 4% of each run, Pallas kernels for 0% -> 5%
where the time goes in v2:
time: 56.9 us; the launch traced here: 56.3 us
  starting transfers between devices  18.3 us (32%)
  Pallas kernels  15 us (26%)
  local copies, waits for them, and re-layouts  11 us (19%)
  waiting for transfers between devices  10.1 us (18%)
  other arithmetic  0.96 us (2%)
  between operations  0.83 us (1%)
    pallas_call x3, Pallas kernels, call(): pl.pallas_call(body, in_specs=[pl.BlockSpec(memory_space=pltpu.SMEM)] * s...  15 us
    all_to_all x1, starting transfers between devices, local(): kv = lax.all_to_all(to_send, both, 0, 0, tiled=True)  7.04 us
    unnamed x25, local copies, waits for them, and re-layouts  6.73 us
    all_to_all x1, waiting for transfers between devices, local(): kv = lax.all_to_all(to_send, both, 0, 0, tiled=True)  6.19 us
    all_to_all x1, starting transfers between devices, local(): arrived = lax.all_to_all(terms, both, 0, 0, tiled=True)  4.53 us
    ppermute x1, starting transfers between devices, local(): lax.ppermute(resp_kv[:, resp_dev - BACK:], 'group', [(i, i + 1) for i in...  4.5 us
    ppermute x1, waiting for transfers between devices, local(): lax.ppermute(local_terms[:, :BACK].astype(BF), 'group', [(i, i - 1) for i...  3.28 us
    ppermute x1, starting transfers between devices, local(): lax.ppermute(local_terms[:, :BACK].astype(BF), 'group', [(i, i - 1) for i...  2.23 us
  transfers between devices with their start and end apart: 4, of which 3 were waited for; matrix products, arithmetic and copies ran while one was open for 4% of the time, Pallas kernels for 5%

profile of v2, /device:TPU:1, one launch (start us, length us, event | category | flops | bytes accessed | tf_op | source)
XLA Modules:
  0.0 56.3 jit_solution(958714301037113485)
XLA Ops:
  0.6 0.0 copy-start.9
  0.6 0.8 %slice.38 = bf16[2,64,128]{2,1,0:T(8,128)(2,1)S(1)} slice(bf16[2,256,128]{2,1,0:T(8,128)(2,1)} %param.10), slice={[0:2], [192:256], [0:128]} | slice | bytes 65536 | tf_op jit(solution)/shard_map/slice | solution.py:214
  1.4 4.5 %collective-permute-start = (bf16[2,64,128]{2,1,0:T(8,128)(2,1)S(1)}, bf16[2,64,128]{2,1,0:T(8,128)(2,1)S(1)}, u32[]{:S(2)}, u32[]{:S(2)}) collective-permute-start(bf16[2,64,128]{2,1,0:T(8,128)(2,1)S(1)} %slice.38), channel_id=1, source_target_pairs={{0,4},{4,8},{8,12},{12,16},{16,20},{20,24},{24,28},{1,5},{5,9},{9,... | collective-permute-start | bytes 98312 | tf_op jit(solution)/shard_map/ppermute | solution.py:213
  5.9 0.0 copy-done.9
  6.0 0.9 %broadcast_in_dim.10 = bf16[8,4,2,32,128]{4,3,2,1,0:T(8,128)(2,1)} broadcast(bf16[4,2,32,128]{3,2,1,0:T(8,128)(2,1)S(1)} %copy.15), dimensions={1,2,3,4} | broadcast | bytes 589824 | tf_op jit(solution)/shard_map/broadcast_in_dim | solution.py:211
  6.9 0.0 copy-start.8
  6.9 7.0 %all-to-all-start = ((bf16[32,2,32,128]{3,2,1,0:T(8,128)(2,1)}), bf16[32,2,32,128]{3,2,1,0:T(8,128)(2,1)S(1)}, u32[]{:S(2)}, u32[]{:S(2)}) async-start(bf16[32,2,32,128]{3,2,1,0:T(8,128)(2,1)} %bitcast.2), calls=%async_computation | async-start | bytes 1048576 | tf_op jit(solution)/shard_map/all_to_all | solution.py:212
  14.0 0.0 copy-start.10
  14.0 0.7 %copy-done.10 = s32[2048]{0:T(1024)S(1)} copy-done((s32[2048]{0:T(1024)S(1)}, s32[2048]{0:T(1024)}, u32[]{:S(2)}) %copy-start.10) | copy-done | bytes 8216
  14.7 0.1 pad_dynamic-slice_fusion
  14.8 0.1 fusion.1
  14.8 0.1 slice.46
  14.9 0.1 slice.42
  15.0 0.5 copy-done.11
  15.5 0.0 slice-start.1
  15.5 0.7 %slice-done.1 = s32[192]{0:T(256)S(1)} async-done(((s32[320]{0:T(512)}), s32[192]{0:T(256)S(1)}, s32[]{:S(2)}) %slice-start.1) | async-done | bytes 792 | tf_op jit(solution)/shard_map/slice | solution.py:224
  16.2 0.0 copy-start
  16.2 0.0 copy-start.1
  16.2 0.2 and_select_fusion
  16.4 0.0 collective-permute-done
  16.4 0.0 copy-done.8
  16.4 0.8 %copy-done = bf16[256,896]{1,0:T(8,128)(2,1)S(1)} copy-done((bf16[256,896]{1,0:T(8,128)(2,1)S(1)}, bf16[256,896]{1,0:T(8,128)(2,1)}, u32[]{:S(2)}) %copy-start) | copy-done | bytes 458776
  17.2 0.1 copy-done.1
  17.3 0.6 %local_forward.1 = (bf16[2,192,896]{2,1,0:T(8,128)(2,1)S(1)}, f32[7,8,256]{2,1,0:T(8,128)S(1)}) custom-call(bf16[2,320,128]{2,1,0:T(8,128)(2,1)S(1)} %constant_dynamic-update-slice_fusion.lkv_ref, f32[2,192,128]{2,1,0:T(8,128)S(1)} %pad_maximum_fusion.bias_ref, bf16[256,896]{1,0:T(8,128)(2,1)S(1)} %copy-done, bf16[256,896]{1,0:T(8,128)(2,1)S(1)} %copy-done.1), custom_call_target="tpu_custom_call" | custom-call | flops 176160768 | bytes 4194304 | tf_op jit(solution)/shard_map/local_forward/pallas_call | solution.py:188
  18.0 0.0 copy-start.2
  18.0 0.8 %copy-done.2 = bf16[2,192,896]{2,1,0:T(8,128)(2,1)} copy-done((bf16[2,192,896]{2,1,0:T(8,128)(2,1)}, bf16[2,192,896]{2,1,0:T(8,128)(2,1)S(1)}, u32[]{:S(2)}) %copy-start.2) | copy-done | bytes 688152
  18.8 6.2 %all-to-all-done.kv_ref = bf16[32,2,32,128]{3,2,1,0:T(8,128)(2,1)S(1)} async-done(((bf16[32,2,32,128]{3,2,1,0:T(8,128)(2,1)}), bf16[32,2,32,128]{3,2,1,0:T(8,128)(2,1)S(1)}, u32[]{:S(2)}, u32[]{:S(2)}) %all-to-all-start) | async-done | bytes 524320 | tf_op jit(solution)/shard_map/all_to_all | solution.py:212
  25.0 0.0 copy-start.5
  25.0 0.9 %copy-done.5 = bf16[128,896]{1,0:T(8,128)(2,1)S(1)} copy-done((bf16[128,896]{1,0:T(8,128)(2,1)S(1)}, bf16[128,896]{1,0:T(8,128)(2,1)}, u32[]{:S(2)}) %copy-start.5) | copy-done | bytes 229400
  26.0 0.0 copy-start.6
  26.0 0.9 %copy-done.6 = bf16[128,896]{1,0:T(8,128)(2,1)S(1)} copy-done((bf16[128,896]{1,0:T(8,128)(2,1)S(1)}, bf16[128,896]{1,0:T(8,128)(2,1)}, u32[]{:S(2)}) %copy-start.6) | copy-done | bytes 229400
  26.9 12.2 %prefix_attention.1 = (f32[256,896]{1,0:T(8,128)S(1)}, bf16[128,896]{1,0:T(8,128)(2,1)}, f32[256,896]{1,0:T(8,128)S(1)}, bf16[128,896]{1,0:T(8,128)(2,1)}, f32[7...) custom-call(s32[1]{0:T(128)} %bitcast.first_ref, bf16[32,2,32,128]{3,2,1,0:T(8,128)(2,1)S(1)} %all-to-all-done.kv_ref, ...), custom_call_target="tpu_custom_call" | custom-call | flops 4227858432 | bytes 4194304 | tf_op jit(solution)/shard_map/prefix_attention/pallas_call | solution.py:188
  39.1 0.0 copy-start.4
  39.1 0.8 %copy-done.4 = bf16[32,2,32,128]{3,2,1,0:T(8,128)(2,1)} copy-done((bf16[32,2,32,128]{3,2,1,0:T(8,128)(2,1)}, bf16[32,2,32,128]{3,2,1,0:T(8,128)(2,1)S(1)}, u32[]{:S(2)}) %copy-start.4) | copy-done | bytes 524312
  39.9 4.5 %all-to-all-start.1 = ((bf16[32,2,32,128]{3,2,1,0:T(8,128)(2,1)}), bf16[32,2,32,128]{3,2,1,0:T(8,128)(2,1)S(1)}, u32[]{:S(2)}, u32[]{:S(2)}) async-start(bf16[32,2,32,128]{3,2,1,0:T(8,128)(2,1)} %copy-done.4), calls=%async_computation.1 | async-start | bytes 1048576 | tf_op jit(solution)/shard_map/all_to_all | solution.py:254
  44.4 0.0 copy-start.3
  44.5 1.1 %copy-done.3 = bf16[2,192,896]{2,1,0:T(8,128)(2,1)S(1)} copy-done((bf16[2,192,896]{2,1,0:T(8,128)(2,1)S(1)}, bf16[2,192,896]{2,1,0:T(8,128)(2,1)}, u32[]{:S(2)}) %copy-start.3) | copy-done | bytes 688152
  45.5 2.2 %local_backward.1 = (f32[2,320,128]{2,1,0:T(8,128)S(1)}, bf16[256,896]{1,0:T(8,128)(2,1)}, bf16[256,896]{1,0:T(8,128)(2,1)}) custom-call(bf16[2,320,128]{2,1,0:T(8,128)(2,1)S(1)} %constant_dynamic-update-slice_fusion.lkv_ref, bf16[2,192,896]{2,1,0:T(8,128)(2,1)S(1)} %copy-done.3, f32[7,8,256]{2,1,0:T(8,128)S(1)} %get-tuple-element.20.fs_ref, ...), custom_call_target="tpu_custom_call" | custom-call | flops 440401920 | bytes 4194304 | tf_op jit(solution)/shard_map/local_backward/pallas_call | solution.py:188
  47.8 0.0 copy-start.7
  47.8 2.2 %collective-permute-start.1 = (bf16[2,64,128]{2,1,0:T(8,128)(2,1)S(1)}, bf16[2,64,128]{2,1,0:T(8,128)(2,1)S(1)}, u32[]{:S(2)}, u32[]{:S(2)}) collective-permute-start(bf16[2,64,128]{2,1,0:T(8,128)(2,1)S(1)} %slice.51), channel_id=1, source_target_pairs={{4,0},{8,4},{12,8},{16,12},{20,16},{24,20},{28,24},{5,1},{9,5},{13... | collective-permute-start | bytes 98312 | tf_op jit(solution)/shard_map/ppermute | solution.py:261
  50.0 0.0 copy-done.7
  50.1 3.3 %collective-permute-done.1 = bf16[2,64,128]{2,1,0:T(8,128)(2,1)S(1)} collective-permute-done((bf16[2,64,128]{2,1,0:T(8,128)(2,1)S(1)}, bf16[2,64,128]{2,1,0:T(8,128)(2,1)S(1)}, u32[]{:S(2)}, u32[]{:S(2)}) %collective-permute-start.1) | collective-permute-done | bytes 32800 | tf_op jit(solution)/shard_map/ppermute | solution.py:261
  53.3 0.0 slice-start
  53.3 0.9 %slice-done = bf16[2,192,128]{2,1,0:T(8,128)(2,1)S(1)} async-done(((bf16[2,320,128]{2,1,0:T(8,128)(2,1)}), bf16[2,192,128]{2,1,0:T(8,128)(2,1)S(1)}, s32[]{:S(2)}) %slice-start) | async-done | bytes 98328 | tf_op jit(solution)/shard_map/slice | solution.py:265
  54.2 0.7 %pad_maximum_fusion.1 = bf16[2,256,128]{2,1,0:T(8,128)(2,1)} fusion(bf16[2,64,128]{2,1,0:T(8,128)(2,1)S(1)} %add_convert_fusion, bf16[2,192,128]{2,1,0:T(8,128)(2,1)S(1)} %slice-done), kind=kLoop, calls=%fused_computation.1 | loop fusion | flops 262144 | bytes 262144 | tf_op jit(solution)/shard_map/concatenate | solution.py:264
  54.9 0.7 %all-to-all-done.1 = bf16[32,2,32,128]{3,2,1,0:T(8,128)(2,1)S(1)} async-done(((bf16[32,2,32,128]{3,2,1,0:T(8,128)(2,1)}), bf16[32,2,32,128]{3,2,1,0:T(8,128)(2,1)S(1)}, u32[]{:S(2)}, u32[]{:S(2)}) %all-to-all-start.1) | async-done | bytes 524320 | tf_op jit(solution)/shard_map/all_to_all | solution.py:254
  55.6 0.1 reduce_sum.12
  55.6 0.6 %copy_bitcast_fusion = bf16[2,32,512]{2,1,0:T(8,128)(2,1)} fusion(bf16[4,2,32,128]{3,2,1,0:T(8,128)(2,1)S(1)} %reduce_sum.12), kind=kLoop, calls=%fused_computation.4 | loop fusion | bytes 131072 | tf_op jit(solution)/shard_map/reshape | solution.py:268
  (13 shorter events, 0.1 us)
Async XLA Ops:
  0.6 5.3 %copy-start.9 = (bf16[2,32,512]{2,1,0:T(8,128)(2,1)S(1)}, bf16[2,32,512]{2,1,0:T(8,128)(2,1)}, u32[]{:S(2)}) copy-start(bf16[2,32,512]{2,1,0:T(8,128)(2,1)} %param.8) | copy-start | bytes 196612
  1.4 14.9 %collective-permute-start = (bf16[2,64,128]{2,1,0:T(8,128)(2,1)S(1)}, bf16[2,64,128]{2,1,0:T(8,128)(2,1)S(1)}, u32[]{:S(2)}, u32[]{:S(2)}) collective-permute-start(bf16[2,64,128]{2,1,0:T(8,128)(2,1)S(1)} %slice.38), channel_id=1, source_target_pairs={{0,4},{4,8},{8,12},{12,16},{16,20},{20,24},{24,28},{1,5},{5,9},{9,... | collective-permute-start | bytes 98312 | tf_op jit(solution)/shard_map/ppermute | solution.py:213
  6.9 9.5 %copy-start.8 = (bf16[2,256,128]{2,1,0:T(8,128)(2,1)S(1)}, bf16[2,256,128]{2,1,0:T(8,128)(2,1)}, u32[]{:S(2)}) copy-start(bf16[2,256,128]{2,1,0:T(8,128)(2,1)} %param.10) | copy-start | bytes 393220
  6.9 18.1 %all-to-all-start = ((bf16[32,2,32,128]{3,2,1,0:T(8,128)(2,1)}), bf16[32,2,32,128]{3,2,1,0:T(8,128)(2,1)S(1)}, u32[]{:S(2)}, u32[]{:S(2)}) async-start(bf16[32,2,32,128]{3,2,1,0:T(8,128)(2,1)} %bitcast.2), calls=%async_computation | async-start | bytes 1048576 | tf_op jit(solution)/shard_map/all_to_all | solution.py:212
  14.0 0.7 %copy-start.10 = (s32[2048]{0:T(1024)S(1)}, s32[2048]{0:T(1024)}, u32[]{:S(2)}) copy-start(s32[2048]{0:T(1024)} %param.11) | copy-start | bytes 24580
  14.9 0.6 %copy-start.11 = (s32[320]{0:T(512)}, s32[320]{0:T(512)S(1)}, u32[]{:S(2)}) copy-start(s32[320]{0:T(512)S(1)} %iota.5) | copy-start | bytes 3844
  15.5 0.7 %slice-start.1 = ((s32[320]{0:T(512)}), s32[192]{0:T(256)S(1)}, s32[]{:S(2)}) async-start(s32[320]{0:T(512)} %copy-done.11), calls=%async_computation.3 | async-start | bytes 2048 | tf_op jit(solution)/shard_map/slice | solution.py:224
  16.2 1.0 %copy-start = (bf16[256,896]{1,0:T(8,128)(2,1)S(1)}, bf16[256,896]{1,0:T(8,128)(2,1)}, u32[]{:S(2)}) copy-start(bf16[256,896]{1,0:T(8,128)(2,1)} %q_ref.3) | copy-start | bytes 1376260
  16.2 1.2 %copy-start.1 = (bf16[256,896]{1,0:T(8,128)(2,1)S(1)}, bf16[256,896]{1,0:T(8,128)(2,1)}, u32[]{:S(2)}) copy-start(bf16[256,896]{1,0:T(8,128)(2,1)} %g_ref.3) | copy-start | bytes 1376260
  18.0 0.9 %copy-start.2 = (bf16[2,192,896]{2,1,0:T(8,128)(2,1)}, bf16[2,192,896]{2,1,0:T(8,128)(2,1)S(1)}, u32[]{:S(2)}) copy-start(bf16[2,192,896]{2,1,0:T(8,128)(2,1)S(1)} %get-tuple-element.19.p_ref) | copy-start | bytes 2064388
  25.0 0.9 %copy-start.5 = (bf16[128,896]{1,0:T(8,128)(2,1)S(1)}, bf16[128,896]{1,0:T(8,128)(2,1)}, u32[]{:S(2)}) copy-start(bf16[128,896]{1,0:T(8,128)(2,1)} %qp_ref.1) | copy-start | bytes 688132
  26.0 0.9 %copy-start.6 = (bf16[128,896]{1,0:T(8,128)(2,1)S(1)}, bf16[128,896]{1,0:T(8,128)(2,1)}, u32[]{:S(2)}) copy-start(bf16[128,896]{1,0:T(8,128)(2,1)} %gp_ref.1) | copy-start | bytes 688132
  39.1 0.8 %copy-start.4 = (bf16[32,2,32,128]{3,2,1,0:T(8,128)(2,1)}, bf16[32,2,32,128]{3,2,1,0:T(8,128)(2,1)S(1)}, u32[]{:S(2)}) copy-start(bf16[32,2,32,128]{3,2,1,0:T(8,128)(2,1)S(1)} %get-tuple-element.26) | copy-start | bytes 1572868
  39.9 15.7 %all-to-all-start.1 = ((bf16[32,2,32,128]{3,2,1,0:T(8,128)(2,1)}), bf16[32,2,32,128]{3,2,1,0:T(8,128)(2,1)S(1)}, u32[]{:S(2)}, u32[]{:S(2)}) async-start(bf16[32,2,32,128]{3,2,1,0:T(8,128)(2,1)} %copy-done.4), calls=%async_computation.1 | async-start | bytes 1048576 | tf_op jit(solution)/shard_map/all_to_all | solution.py:254
  44.4 1.1 %copy-start.3 = (bf16[2,192,896]{2,1,0:T(8,128)(2,1)S(1)}, bf16[2,192,896]{2,1,0:T(8,128)(2,1)}, u32[]{:S(2)}) copy-start(bf16[2,192,896]{2,1,0:T(8,128)(2,1)} %copy-done.2) | copy-start | bytes 2064388
  47.8 2.3 %copy-start.7 = (bf16[2,320,128]{2,1,0:T(8,128)(2,1)}, bf16[2,320,128]{2,1,0:T(8,128)(2,1)S(1)}, u32[]{:S(2)}) copy-start(bf16[2,320,128]{2,1,0:T(8,128)(2,1)S(1)} %convert.9) | copy-start | bytes 491524
  47.8 5.5 %collective-permute-start.1 = (bf16[2,64,128]{2,1,0:T(8,128)(2,1)S(1)}, bf16[2,64,128]{2,1,0:T(8,128)(2,1)S(1)}, u32[]{:S(2)}, u32[]{:S(2)}) collective-permute-start(bf16[2,64,128]{2,1,0:T(8,128)(2,1)S(1)} %slice.51), channel_id=1, source_target_pairs={{4,0},{8,4},{12,8},{16,12},{20,16},{24,20},{28,24},{5,1},{9,5},{13... | collective-permute-start | bytes 98312 | tf_op jit(solution)/shard_map/ppermute | solution.py:261
  53.3 0.9 %slice-start = ((bf16[2,320,128]{2,1,0:T(8,128)(2,1)}), bf16[2,192,128]{2,1,0:T(8,128)(2,1)S(1)}, s32[]{:S(2)}) async-start(bf16[2,320,128]{2,1,0:T(8,128)(2,1)} %copy-done.7), calls=%async_computation.2 | async-start | bytes 196608 | tf_op jit(solution)/shard_map/slice | solution.py:265

commit v3 on v2

v3 whole, which is shorter than its diff:
```python
import math

import jax
import jax.numpy as jnp
from jax import lax
from jax.experimental import pallas as pl
from jax.experimental.pallas import tpu as pltpu
from jax.sharding import Mesh
from jax.sharding import PartitionSpec as P

D = 128
BF = jnp.bfloat16
F = jnp.float32
SCALE = D**-0.5
SCALE2 = SCALE * math.log2(math.e)
MASKED = -1e30
GROUP = ("chip", "core")
BACK = 64
NT = (((1,), (1,)), ((), ()))
TN = (((0,), (0,)), ((), ()))
NN = (((1,), (0,)), ((), ()))
CHUNK = 1024
UNIT = 2


def mm(a, b, dims):
    return lax.dot_general(a, b, dims, preferred_element_type=F)


def fold(x, op):
    return op(x.reshape(x.shape[0] // 8, 8, x.shape[1]), 0)


def stack_heads(ref, rows):
    return jnp.concatenate([ref[rows, i : i + D] for i in range(0, ref.shape[1], D)], 0)


def spread(kv_ref, out_ref, buffer, sem):
    count = buffer.shape[0]
    for t in range(count):
        buffer[t] = kv_ref[:, :, t * D : (t + 1) * D]
    copies = [
        pltpu.make_async_copy(buffer, out_ref.at[i : i + count], sem.at[i // count])
        for i in range(0, out_ref.shape[0], count)
    ]
    for copy in copies:
        copy.start()
    for copy in copies:
        copy.wait()


def gathered_sum(in_ref, out_ref):
    count = out_ref.shape[2] // D
    for t in range(count):
        total = in_ref[t].astype(F)
        for i in range(t + count, in_ref.shape[0], count):
            total = total + in_ref[i].astype(F)
        out_ref[:, :, t * D : (t + 1) * D] = total.astype(BF)


def local_parts(segs_ref, prior_ref, kv_ref, q_ref, g_ref):
    half = q_ref.shape[0] // 2
    start = pl.multiple_of(lax.axis_index(GROUP) * 2 * half, 2 * half)
    before = segs_ref[:, pl.ds(pl.multiple_of(jnp.maximum(start - half, 0), half), half)]
    before = jnp.where(start > 0, before, -1)[:, half - BACK :]
    segs = jnp.concatenate([before, segs_ref[:, pl.ds(start, 2 * half)]], 1).astype(F)
    by_key = jnp.broadcast_to(segs, (half, segs.shape[1])).T
    for i in range(2):
        rows = slice(i * half, (i + 1) * half)
        span = slice(i * half, i * half + half + BACK)
        k = jnp.concatenate([prior_ref[0], kv_ref[0]], 0)[span]
        v = jnp.concatenate([prior_ref[1], kv_ref[1]], 0)[span]
        behind = lax.broadcasted_iota(jnp.int32, (half + BACK, half), 0) - lax.broadcasted_iota(
            jnp.int32, (half + BACK, half), 1
        )
        same = by_key[span] == segs[:, i * half + BACK : (i + 1) * half + BACK]
        bias = jnp.where(same & (behind <= BACK), 0.0, MASKED)
        q = stack_heads(q_ref, rows)
        g = stack_heads(g_ref, rows)
        s = mm(k, q, NT) + jnp.concatenate([bias] * (q_ref.shape[1] // D), 1)
        yield rows, k, v, q, g, s


def local_forward(segs_ref, prior_ref, kv_ref, q_ref, g_ref, stat_ref):
    heads = q_ref.shape[1] // D
    for rows, k, v, q, g, s in local_parts(segs_ref, prior_ref, kv_ref, q_ref, g_ref):
        m = jnp.max(s, 0, keepdims=True)
        p = jnp.exp2((s - m) * SCALE2)
        total = jnp.sum(p, 0, keepdims=True)
        mix = jnp.sum(p * mm(v, g, NT), 0, keepdims=True)
        for h in range(heads):
            c = slice(h * 128, (h + 1) * 128)
            stat_ref[h, 0:1, rows] = m[:, c]
            stat_ref[h, 1:2, rows] = total[:, c]
            stat_ref[h, 2:3, rows] = mix[:, c]


def local_backward(
    segs_ref, prior_ref, kv_ref, q_ref, g_ref, stat_ref, fs_ref, o1_ref, dq1_ref,
    back_ref, rest_ref, dkv_ref, o_ref, dq_ref,
):
    heads = q_ref.shape[1] // D
    terms = []
    for rows, k, v, q, g, s in local_parts(segs_ref, prior_ref, kv_ref, q_ref, g_ref):
        m = jnp.concatenate([stat_ref[h, 0:1, rows] for h in range(heads)], 1)
        f = jnp.concatenate([fs_ref[h, 0:1, rows] for h in range(heads)], 1)
        delta = jnp.concatenate([fs_ref[h, 1:2, rows] for h in range(heads)], 1)
        wf = jnp.exp2((s - m) * SCALE2) * f
        w = wf.astype(BF)
        ds = (wf * (mm(v, g, NT) - delta)).astype(BF)
        terms.append((mm(ds, q, NN) * SCALE, mm(w, g, NN)))
        o = mm(w, v, TN)
        dq = mm(ds, k, TN) * SCALE
        for h in range(heads):
            c = slice(h * D, (h + 1) * D)
            r = slice(h * 128, (h + 1) * 128)
            o_ref[rows, c] = (o[r] + o1_ref[rows, c].astype(F)).astype(BF)
            dq_ref[rows, c] = (dq[r] + dq1_ref[rows, c].astype(F)).astype(BF)
    for x in range(2):
        a, b = terms[0][x], terms[1][x]
        back_ref[x] = a[0:64].astype(BF)
        dkv_ref[x, 0:64] = a[64:128].astype(BF)
        dkv_ref[x, 64:128] = (a[128:192] + b[0:64]).astype(BF)
        dkv_ref[x, 128:192] = b[64:128].astype(BF)
        dkv_ref[x, 192:256] = b[128:192].astype(BF)
        rest_ref[x] = b[128:192]


def prefix_attention(
    own_ref, other_ref, stat_ref, qr_ref, gr_ref, qp_ref, gp_ref,
    or_ref, op_ref, dqr_ref, dqp_ref, fs_ref, terms_ref,
    k_s, v_s, kt_s, vt_s, s_s, d_s, acck, accv,
):
    heads = qr_ref.shape[1] // D
    keys = k_s.shape[0]
    slots = s_s.shape[0]
    each = keys // 8
    core = lax.axis_index("core")
    for x in range(4):
        for ref, c in ((own_ref, core), (other_ref, 1 - core)):
            at = pl.ds(pl.multiple_of((2 * x + c) * each, each), each)
            k_s[at, :] = ref[4 * x : 4 * x + 4, 0].reshape(each, D)
            v_s[at, :] = ref[4 * x : 4 * x + 4, 1].reshape(each, D)
    kt_s[...] = k_s[...].T
    vt_s[...] = v_s[...].T
    first = lax.axis_index(GROUP) * qp_ref.shape[0]
    ahead = lax.broadcasted_iota(jnp.int32, (CHUNK, 128), 0) - lax.broadcasted_iota(
        jnp.int32, (CHUNK, 128), 1
    )
    blocks = [(h, slice(i * 128, i * 128 + 128)) for h in range(heads) for i in range(2)]
    blocks += [(h, None) for h in range(heads)]
    units = [blocks[i : i + UNIT] for i in range(0, len(blocks), UNIT)]
    held = {}

    def load(resp, prompt, unit):
        c = lambda h: slice(h * D, (h + 1) * D)
        return jnp.concatenate([prompt[:, c(h)] if r is None else resp[r, c(h)] for h, r in unit], 0)

    def by_block(unit, x, near):
        parts = []
        for i, (h, r) in enumerate(unit):
            part = x[:, i * 128 : i * 128 + 128]
            parts.append(part if r is None else near(h, r, part))
        return jnp.concatenate(parts, 1)

    def scores(u, k0):
        unit = units[u]
        if k0 == 0:
            held[u] = {"q": load(qr_ref, qp_ref, unit), "g": load(gr_ref, gp_ref, unit)}
        d = held[u]
        at = slice(k0, k0 + CHUNK)
        s = mm(k_s[at, :], d["q"], NT)
        if unit[-1][1] is None:
            cut = [s[:, i * 128 : i * 128 + 128] for i in range(len(unit))]
            seen = ahead <= first - k0
            cut = [jnp.where(seen, x, MASKED) if r is None else x for x, (h, r) in zip(cut, unit)]
            s = jnp.concatenate(cut, 1)
        cols = slice(0, len(unit) * 128)
        s_s[u % slots, at, cols] = s
        peak = fold(s, jnp.max)
        d["m"] = jnp.maximum(d["m"], peak) if k0 else peak
        d_s[u % slots, at, cols] = mm(v_s[at, :], d["g"], NT)

    def raised(u, k0):
        unit = units[u]
        d = held[u]
        cols = slice(0, len(unit) * 128)
        if k0 == 0:
            m = jnp.max(d["m"], 0, keepdims=True)
            d["m"] = by_block(unit, m, lambda h, r, x: jnp.maximum(x, stat_ref[h, 0:1, r]))
            peak = by_block(unit, d["m"], lambda h, r, x: stat_ref[h, 0:1, r])
            d["f"] = jnp.exp2((peak - d["m"]) * SCALE2)
            d["m"] = d["m"] * SCALE2
        at = slice(k0, k0 + CHUNK)
        p = jnp.exp2(s_s[u % slots, at, cols] * SCALE2 - d["m"])
        s_s[u % slots, at, cols] = p
        total = fold(p, jnp.sum)
        mix = fold(p * d_s[u % slots, at, cols], jnp.sum)
        d["l"] = d["l"] + total if k0 else total
        d["t"] = d["t"] + mix if k0 else mix

    def products(u, k0):
        unit = units[u]
        d = held[u]
        cols = slice(0, len(unit) * 128)
        if k0 == 0:
            f = d["f"]
            l = jnp.sum(d["l"], 0, keepdims=True)
            t = jnp.sum(d["t"], 0, keepdims=True)
            l = l + f * by_block(unit, jnp.zeros_like(l), lambda h, r, x: stat_ref[h, 1:2, r])
            t = t + f * by_block(unit, jnp.zeros_like(t), lambda h, r, x: stat_ref[h, 2:3, r])
            d["inv"] = 1.0 / l
            d["delta"] = t * d["inv"]
            f = f * d["inv"]
            for i, (h, r) in enumerate(unit):
                if r is not None:
                    fs_ref[h, 0:1, r] = f[:, i * 128 : i * 128 + 128]
                    fs_ref[h, 1:2, r] = d["delta"][:, i * 128 : i * 128 + 128]
        at = slice(k0, k0 + CHUNK)
        w = s_s[u % slots, at, cols] * d["inv"]
        ds = (w * (d_s[u % slots, at, cols] - d["delta"])).astype(BF)
        w = w.astype(BF)
        o = mm(vt_s[:, at], w, NN)
        dq = mm(kt_s[:, at], ds, NN)
        d["o"] = d["o"] + o if k0 else o
        d["dq"] = d["dq"] + dq if k0 else dq
        dv = mm(w, d["g"], NN)
        dk = mm(ds, d["q"], NN)
        accv[at, :] = accv[at, :] + dv if u else dv
        acck[at, :] = acck[at, :] + dk if u else dk
        if k0 + CHUNK == keys:
            o = d["o"].T
            dq = d["dq"].T * SCALE
            for i, (h, r) in enumerate(unit):
                c = slice(h * D, (h + 1) * D)
                a = slice(i * 128, i * 128 + 128)
                if r is None:
                    op_ref[:, c] = o[a].astype(BF)
                    dqp_ref[:, c] = dq[a].astype(BF)
                else:
                    or_ref[r, c] = o[a].astype(BF)
                    dqr_ref[r, c] = dq[a].astype(BF)
            del held[u]

    for i in range(len(units) + 2):
        for k0 in range(0, keys, CHUNK):
            for late, stage in enumerate((scores, raised, products)):
                if 0 <= i - late < len(units):
                    stage(i - late, k0)
    terms_ref[:, 0] = (acck[...] * SCALE).astype(BF).reshape(-1, keys // terms_ref.shape[0], D)
    terms_ref[:, 1] = accv[...].astype(BF).reshape(-1, keys // terms_ref.shape[0], D)


def shape(*dims, dtype=BF):
    return jax.ShapeDtypeStruct(dims, dtype)


def call(body, outs, operands, flops, scratch=(), grant=16):
    vmem = pl.BlockSpec(memory_space=pltpu.VMEM)
    return pl.pallas_call(
        body,
        in_specs=[vmem] * len(operands),
        out_specs=[vmem] * len(outs),
        out_shape=outs,
        scratch_shapes=scratch,
        compiler_params=pltpu.CompilerParams(vmem_limit_bytes=grant * 2**20),
        cost_estimate=pl.CostEstimate(flops=flops, bytes_accessed=4 * 2**20, transcendentals=0),
        name=body.__name__,
    )(*operands)


def local(prompt_q, prefix_kv, resp_q, resp_kv, resp_segs, grad_prompt_out, grad_resp_out):
    groups = lax.axis_size(GROUP)
    tensors = lax.axis_size("tensor")
    group_rank = lax.axis_index(GROUP)
    rows = prefix_kv.shape[1]
    resp_dev = resp_q.shape[0]
    prompt_dev = prompt_q.shape[0]
    keys = rows * groups * tensors
    both = GROUP + ("tensor",)

    chips = groups // 2
    vm = pltpu.VMEM
    to_send = pl.pallas_call(
        spread,
        in_specs=[pl.BlockSpec(memory_space=vm)],
        out_specs=pl.BlockSpec(memory_space=pl.ANY),
        out_shape=shape(chips * tensors, 2, rows, D),
        scratch_shapes=[vm((tensors, 2, rows, D), BF), pltpu.SemaphoreType.DMA((chips,))],
        cost_estimate=pl.CostEstimate(flops=0, bytes_accessed=2**18, transcendentals=0),
        name="spread",
    )(prefix_kv)
    to_send, held_kv = lax.optimization_barrier((to_send, resp_kv))
    tail = held_kv[:, resp_dev - BACK :]
    own = lax.all_to_all(to_send, ("chip", "tensor"), 0, 0, tiled=True)

    prior = lax.ppermute(tail, GROUP, [(i, i + 1) for i in range(groups - 1)])

    own, prior = lax.optimization_barrier((own, prior))
    other = lax.ppermute(own, "core", [(0, 1), (1, 0)])

    width = resp_q.shape[1]
    heads = width // D
    rows_all = resp_dev + prompt_dev
    work = 2 * D * heads
    near = (resp_segs.reshape(1, -1), prior, resp_kv, resp_q, grad_resp_out)
    (stats,) = call(local_forward, [shape(heads, 8, resp_dev, dtype=F)], near, work * 2 * 192 * resp_dev)
    wide = (resp_dev, width)
    out1, prompt_out, dq1, grad_prompt_q, factors, terms = call(
        prefix_attention,
        [
            shape(*wide), shape(prompt_dev, width), shape(*wide), shape(prompt_dev, width),
            shape(heads, 8, resp_dev, dtype=F), shape(groups * tensors, 2, rows, D),
        ],
        (own, other, stats, resp_q, grad_resp_out, prompt_q, grad_prompt_out),
        work * 6 * keys * rows_all,
        [vm((keys, D), BF), vm((keys, D), BF), vm((D, keys), BF), vm((D, keys), BF)]
        + [vm((3, keys, UNIT * 128), F)] * 2
        + [vm((keys, D), F)] * 2,
        24,
    )
    arrived = lax.all_to_all(terms, both, 0, 0, tiled=True)
    back, rest, grad_resp_kv, resp_out, grad_resp_q = call(
        local_backward,
        [shape(2, BACK, D), shape(2, BACK, D, dtype=F), shape(2, resp_dev, D), shape(*wide), shape(*wide)],
        near + (stats, factors, out1, dq1),
        work * 5 * 192 * resp_dev,
    )
    later = lax.ppermute(back, GROUP, [(i, i - 1) for i in range(1, groups)])
    grad_resp_kv = lax.dynamic_update_slice(
        grad_resp_kv, (rest + later.astype(F)).astype(BF), (0, resp_dev - BACK, 0)
    )
    (grad_prefix_kv,) = call(gathered_sum, [shape(2, rows, tensors * D)], (arrived,), 2**20)
    return (prompt_out, resp_out, grad_prompt_q, grad_resp_q, grad_prefix_kv, grad_resp_kv)


def solution(mesh):
    prompts, groups, tensors = mesh.devices.shape
    parts = Mesh(mesh.devices.reshape(prompts, groups // 2, 2, tensors), ("prompt",) + GROUP + ("tensor",))
    wide = P(("prompt",) + GROUP, "tensor")
    cache = P(None, ("prompt",) + GROUP + ("tensor",), None)
    packed = P(None, ("prompt",) + GROUP, "tensor")
    return jax.shard_map(
        local,
        mesh=parts,
        in_specs=(wide, cache, wide, packed, P("prompt"), wide, wide),
        out_specs=(wide, wide, wide, wide, cache, packed),
        check_vma=False,
    )
```

time: 56.9 us -> 50.4 us (0.89)
  local copies, waits for them, and re-layouts: 11 us -> 2.8 us
  starting transfers between devices: 18.3 us -> 21.1 us
  waiting for transfers between devices: 10.1 us -> 8.07 us
  Pallas kernels: 15 us -> 16.6 us
    all_to_all x1, waiting for transfers between devices: 6.19 us -> 1.3 us  [local(): own = lax.all_to_all(to_send, ('chip', 'tensor'), 0, 0, tiled=True)]
    unnamed x25 -> x16, local copies, waits for them, and re-layouts: 6.73 us -> 2.03 us
    slice x11 -> x1, local copies, waits for them, and re-layouts: 2.59 us -> 0.77 us  [local(): tail = held_kv[:, resp_dev - BACK:]]
    ppermute x2 -> x3, starting transfers between devices: 6.73 us -> 8.53 us  [the longest x1 4.38 us: local(): prior = lax.ppermute(tail, GROUP, [(i, i + 1) for i in range(groups - 1)])]
    ppermute x2 -> x3, waiting for transfers between devices: 3.28 us -> 5.06 us  [the longest x1 4.05 us: local(): later = lax.ppermute(back, GROUP, [(i, i - 1) for i in range(1, groups)])]
    pallas_call x3 -> x5, Pallas kernels: 15 us -> 16.6 us  [the longest x4 14.9 us: call(): pl.pallas_call(body, in_specs=[vmem] * len(operands), out_specs=[vmem] *...]
    all_to_all x1, waiting for transfers between devices: 0.68 us -> 1.71 us  [local(): arrived = lax.all_to_all(terms, both, 0, 0, tiled=True)]
    broadcast_in_dim x1 -> x0, local copies, waits for them, and re-layouts: 0.93 us -> none  [local(): jnp.broadcast_to(by_head[None], (groups,) + by_head.shape)]
  transfers between devices with their start and end apart: 4 -> 5, of which waited for: 3 -> 4; matrix products, arithmetic and copies ran while one was open for 4% -> 3% of each run, Pallas kernels for 5% -> 6%
where the time goes in v3:
time: 50.4 us; the launch traced here: 49.9 us
  starting transfers between devices  21.1 us (42%)
  Pallas kernels  16.6 us (33%)
  waiting for transfers between devices  8.07 us (16%)
  local copies, waits for them, and re-layouts  2.8 us (6%)
  between operations  0.73 us (1%)
  other arithmetic  0.63 us (1%)
    pallas_call x4, Pallas kernels, call(): pl.pallas_call(body, in_specs=[vmem] * len(operands), out_specs=[vmem] *...  14.9 us
    all_to_all x1, starting transfers between devices, local(): own = lax.all_to_all(to_send, ('chip', 'tensor'), 0, 0, tiled=True)  7.6 us
    all_to_all x1, starting transfers between devices, local(): arrived = lax.all_to_all(terms, both, 0, 0, tiled=True)  4.99 us
    ppermute x1, starting transfers between devices, local(): prior = lax.ppermute(tail, GROUP, [(i, i + 1) for i in range(groups - 1)])  4.38 us
    ppermute x1, waiting for transfers between devices, local(): later = lax.ppermute(back, GROUP, [(i, i - 1) for i in range(1, groups)])  4.05 us
    ppermute x1, starting transfers between devices, local(): later = lax.ppermute(back, GROUP, [(i, i - 1) for i in range(1, groups)])  2.13 us
    unnamed x16, local copies, waits for them, and re-layouts  2.03 us
    ppermute x1, starting transfers between devices, local(): other = lax.ppermute(own, 'core', [(0, 1), (1, 0)])  2.02 us
  transfers between devices with their start and end apart: 5, of which 4 were waited for; matrix products, arithmetic and copies ran while one was open for 3% of the time, Pallas kernels for 6%

profile of v3, /device:TPU:1, one launch (start us, length us, event | category | flops | bytes accessed | tf_op | source)
XLA Modules:
  0.0 49.9 jit_solution(12121048463324836437)
XLA Ops:
  0.6 0.0 copy-start.1
  0.6 0.0 copy-start
  0.7 1.7 %spread.1 = bf16[16,2,32,128]{3,2,1,0:T(8,128)(2,1)} custom-call(bf16[2,32,512]{2,1,0:T(8,128)(2,1)} %kv_ref.3), custom_call_target="tpu_custom_call" | custom-call | bytes 262144 | tf_op jit(solution)/shard_map/spread/pallas_call | solution.py:284
  2.3 7.6 %all-to-all-start = ((bf16[16,2,32,128]{3,2,1,0:T(8,128)(2,1)}), bf16[16,2,32,128]{3,2,1,0:T(8,128)(2,1)S(1)}, u32[]{:S(2)}, u32[]{:S(2)}) async-start(bf16[16,2,32,128]{3,2,1,0:T(8,128)(2,1)} %spread.1), calls=%async_computation | async-start | bytes 524288 | tf_op jit(solution)/shard_map/all_to_all | solution.py:295
  9.9 0.8 %slice.3 = bf16[2,64,128]{2,1,0:T(8,128)(2,1)S(1)} slice(bf16[2,256,128]{2,1,0:T(8,128)(2,1)} %kv_ref.5), slice={[0:2], [192:256], [0:128]} | slice | bytes 65536 | tf_op jit(solution)/shard_map/slice | solution.py:294
  10.7 4.4 %collective-permute-start = (bf16[2,64,128]{2,1,0:T(8,128)(2,1)S(1)}, bf16[2,64,128]{2,1,0:T(8,128)(2,1)S(1)}, u32[]{:S(2)}, u32[]{:S(2)}) collective-permute-start(bf16[2,64,128]{2,1,0:T(8,128)(2,1)S(1)} %slice.3), channel_id=1, source_target_pairs={{0,4},{4,8},{8,12},{12,16},{16,20},{20,24},{24,28},{1,5},{5,9},{9,... | collective-permute-start | bytes 98312 | tf_op jit(solution)/shard_map/ppermute | solution.py:297
  15.1 1.0 %collective-permute-done.prior_ref = bf16[2,64,128]{2,1,0:T(8,128)(2,1)S(1)} collective-permute-done((bf16[2,64,128]{2,1,0:T(8,128)(2,1)S(1)}, bf16[2,64,128]{2,1,0:T(8,128)(2,1)S(1)}, u32[]{:S(2)}, u32[]{:S(2)}) %collective-permute-start) | collective-permute-done | bytes 32800 | tf_op jit(solution)/shard_map/ppermute | solution.py:297
  16.1 1.3 %all-to-all-done.own_ref = bf16[16,2,32,128]{3,2,1,0:T(8,128)(2,1)S(1)} async-done(((bf16[16,2,32,128]{3,2,1,0:T(8,128)(2,1)}), bf16[16,2,32,128]{3,2,1,0:T(8,128)(2,1)S(1)}, u32[]{:S(2)}, u32[]{:S(2)}) %all-to-all-start) | async-done | bytes 262176 | tf_op jit(solution)/shard_map/all_to_all | solution.py:295
  17.4 2.0 %collective-permute-start.1 = (bf16[16,2,32,128]{3,2,1,0:T(8,128)(2,1)S(1)}, bf16[16,2,32,128]{3,2,1,0:T(8,128)(2,1)S(1)}, u32[]{:S(2)}, u32[]{:S(2)}) collective-permute-start(bf16[16,2,32,128]{3,2,1,0:T(8,128)(2,1)S(1)} %all-to-all-done.own_ref), channel_id=1, source_target_pairs={{0,4},{4,0},{1,5},{5,1},{2,6},{6,2},{3,7},{7,3},{8,12},{12,8},{9,1... | collective-permute-start | bytes 786440 | tf_op jit(solution)/shard_map/ppermute | solution.py:300
  19.4 0.0 copy-done.1
  19.4 0.0 copy-done
  19.4 0.0 copy-start.2
  19.4 0.9 %copy-done.2 = bf16[2,256,128]{2,1,0:T(8,128)(2,1)S(1)} copy-done((bf16[2,256,128]{2,1,0:T(8,128)(2,1)S(1)}, bf16[2,256,128]{2,1,0:T(8,128)(2,1)}, u32[]{:S(2)}) %copy-start.2) | copy-done | bytes 131096
  20.3 0.0 copy-start.4
  20.3 0.7 %copy-done.4 = s32[2048]{0:T(1024)S(1)} copy-done((s32[2048]{0:T(1024)S(1)}, s32[2048]{0:T(1024)}, u32[]{:S(2)}) %copy-start.4) | copy-done | bytes 8216
  21.0 0.0 copy-start.6
  21.0 0.0 copy-start.7
  21.0 0.6 %local_forward.1.stat_ref = f32[7,8,256]{2,1,0:T(8,128)S(1)} custom-call(s32[1,2048]{1,0:T(1,128)S(1)} %bitcast.1, bf16[2,64,128]{2,1,0:T(8,128)(2,1)S(1)} %collective-permute-done.prior_ref, bf16[2,256,128]{2,1,0:T(8,128)(2,1)S(1)} %copy-done.2, bf16[256,896]{1,0:T(8,128)(2,1)S(1)} %copy-done, bf16[256,896]{1,0:T(8,128)(2,1)S(1)} %copy-done.1), custom_call_target="tpu_custom_call" | custom-call | flops 176160768 | bytes 4194304 | tf_op jit(solution)/shard_map/local_forward/pallas_call | solution.py:260
  21.6 0.0 collective-permute-done.1.other_ref
  21.6 0.3 copy-done.6
  21.9 0.1 copy-done.7
  22.0 11.1 %prefix_attention.1 = (bf16[256,896]{1,0:T(8,128)(2,1)S(1)}, bf16[128,896]{1,0:T(8,128)(2,1)}, bf16[256,896]{1,0:T(8,128)(2,1)S(1)}, bf16[128,896]{1,0:T(8,128)(...) custom-call(bf16[16,2,32,128]{3,2,1,0:T(8,128)(2,1)S(1)} %all-to-all-done.own_ref, ...), custom_call_target="tpu_custom_call" | custom-call | flops 4227858432 | bytes 4194304 | tf_op jit(solution)/shard_map/prefix_attention/pallas_call | solution.py:260
  33.2 0.0 copy-start.3
  33.2 0.0 copy-start.5
  33.2 5.0 %all-to-all-start.1 = ((bf16[32,2,32,128]{3,2,1,0:T(8,128)(2,1)}), bf16[32,2,32,128]{3,2,1,0:T(8,128)(2,1)S(1)}, u32[]{:S(2)}, u32[]{:S(2)}) async-start(bf16[32,2,32,128]{3,2,1,0:T(8,128)(2,1)} %get-tuple-element.32), calls=%async_computation.1 | async-start | bytes 1048576 | tf_op jit(solution)/shard_map/all_to_all | solution.py:322
  38.2 0.0 copy-done.3
  38.2 0.0 copy-done.5
  38.2 2.5 %local_backward.1 = (bf16[2,64,128]{2,1,0:T(8,128)(2,1)S(1)}, f32[2,64,128]{2,1,0:T(8,128)S(1)}, bf16[2,256,128]{2,1,0:T(8,128)(2,1)}, bf16[256,896]{1,0:T(8,128)(2,1)}, bf16[256,896]{1,0:T(8,128)(2,1)}) custom-call(s32[1,2048]{1,0:T(1,128)S(1)} %bitcast.2, bf16[2,64,128]{2,1,0:T(8,128)(2,1)S(1)} %collective-permute-done.prior_ref, ...), custom_call_target="tpu_custom_call" | custom-call | flops 440401920 | bytes 4194304 | tf_op jit(solution)/shard_map/local_backward/pallas_call | solution.py:260
  40.7 2.1 %collective-permute-start.2 = (bf16[2,64,128]{2,1,0:T(8,128)(2,1)S(1)}, bf16[2,64,128]{2,1,0:T(8,128)(2,1)S(1)}, u32[]{:S(2)}, u32[]{:S(2)}) collective-permute-start(bf16[2,64,128]{2,1,0:T(8,128)(2,1)S(1)} %get-tuple-element.35), channel_id=1, source_target_pairs={{4,0},{8,4},{12,8},{16,12},{20,16},{24,20},{28,24},{5,1},{9,5},{13... | collective-permute-start | bytes 98312 | tf_op jit(solution)/shard_map/ppermute | solution.py:329
  42.8 4.1 %collective-permute-done.2 = bf16[2,64,128]{2,1,0:T(8,128)(2,1)S(1)} collective-permute-done((bf16[2,64,128]{2,1,0:T(8,128)(2,1)S(1)}, bf16[2,64,128]{2,1,0:T(8,128)(2,1)S(1)}, u32[]{:S(2)}, u32[]{:S(2)}) %collective-permute-start.2) | collective-permute-done | bytes 32800 | tf_op jit(solution)/shard_map/ppermute | solution.py:329
  46.9 0.6 %fusion = bf16[2,256,128]{2,1,0:T(8,128)(2,1)} fusion(bf16[2,256,128]{2,1,0:T(8,128)(2,1)} %get-tuple-element.33, f32[2,64,128]{2,1,0:T(8,128)S(1)} %get-tuple-element.34, bf16[2,64,128]{2,1,0:T(8,128)(2,1)S(1)} %collective-permute-done.2), kind=kLoop, calls=%fused_computation.1 | loop fusion | flops 49152 | bytes 131072 | tf_op jit(solution)/shard_map/dynamic_update_slice | solution.py:330
  47.5 1.7 %all-to-all-done.1.in_ref = bf16[32,2,32,128]{3,2,1,0:T(8,128)(2,1)S(1)} async-done(((bf16[32,2,32,128]{3,2,1,0:T(8,128)(2,1)}), bf16[32,2,32,128]{3,2,1,0:T(8,128)(2,1)S(1)}, u32[]{:S(2)}, u32[]{:S(2)}) %all-to-all-start.1) | async-done | bytes 524320 | tf_op jit(solution)/shard_map/all_to_all | solution.py:322
  49.2 0.7 %gathered_sum.1 = bf16[2,32,512]{2,1,0:T(8,128)(2,1)} custom-call(bf16[32,2,32,128]{3,2,1,0:T(8,128)(2,1)S(1)} %all-to-all-done.1.in_ref), custom_call_target="tpu_custom_call" | custom-call | flops 1048576 | bytes 4194304 | tf_op jit(solution)/shard_map/gathered_sum/pallas_call | solution.py:260
Async XLA Ops:
  0.6 18.8 %copy-start.1 = (bf16[256,896]{1,0:T(8,128)(2,1)S(1)}, bf16[256,896]{1,0:T(8,128)(2,1)}, u32[]{:S(2)}) copy-start(bf16[256,896]{1,0:T(8,128)(2,1)} %g_ref.3) | copy-start | bytes 1376260
  0.6 18.8 %copy-start = (bf16[256,896]{1,0:T(8,128)(2,1)S(1)}, bf16[256,896]{1,0:T(8,128)(2,1)}, u32[]{:S(2)}) copy-start(bf16[256,896]{1,0:T(8,128)(2,1)} %q_ref.3) | copy-start | bytes 1376260
  2.3 15.1 %all-to-all-start = ((bf16[16,2,32,128]{3,2,1,0:T(8,128)(2,1)}), bf16[16,2,32,128]{3,2,1,0:T(8,128)(2,1)S(1)}, u32[]{:S(2)}, u32[]{:S(2)}) async-start(bf16[16,2,32,128]{3,2,1,0:T(8,128)(2,1)} %spread.1), calls=%async_computation | async-start | bytes 524288 | tf_op jit(solution)/shard_map/all_to_all | solution.py:295
  10.7 5.4 %collective-permute-start = (bf16[2,64,128]{2,1,0:T(8,128)(2,1)S(1)}, bf16[2,64,128]{2,1,0:T(8,128)(2,1)S(1)}, u32[]{:S(2)}, u32[]{:S(2)}) collective-permute-start(bf16[2,64,128]{2,1,0:T(8,128)(2,1)S(1)} %slice.3), channel_id=1, source_target_pairs={{0,4},{4,8},{8,12},{12,16},{16,20},{20,24},{24,28},{1,5},{5,9},{9,... | collective-permute-start | bytes 98312 | tf_op jit(solution)/shard_map/ppermute | solution.py:297
  17.4 4.3 %collective-permute-start.1 = (bf16[16,2,32,128]{3,2,1,0:T(8,128)(2,1)S(1)}, bf16[16,2,32,128]{3,2,1,0:T(8,128)(2,1)S(1)}, u32[]{:S(2)}, u32[]{:S(2)}) collective-permute-start(bf16[16,2,32,128]{3,2,1,0:T(8,128)(2,1)S(1)} %all-to-all-done.own_ref), channel_id=1, source_target_pairs={{0,4},{4,0},{1,5},{5,1},{2,6},{6,2},{3,7},{7,3},{8,12},{12,8},{9,1... | collective-permute-start | bytes 786440 | tf_op jit(solution)/shard_map/ppermute | solution.py:300
  19.4 0.9 %copy-start.2 = (bf16[2,256,128]{2,1,0:T(8,128)(2,1)S(1)}, bf16[2,256,128]{2,1,0:T(8,128)(2,1)}, u32[]{:S(2)}) copy-start(bf16[2,256,128]{2,1,0:T(8,128)(2,1)} %kv_ref.5) | copy-start | bytes 393220
  20.3 0.7 %copy-start.4 = (s32[2048]{0:T(1024)S(1)}, s32[2048]{0:T(1024)}, u32[]{:S(2)}) copy-start(s32[2048]{0:T(1024)} %param.11) | copy-start | bytes 24580
  21.0 0.9 %copy-start.6 = (bf16[128,896]{1,0:T(8,128)(2,1)S(1)}, bf16[128,896]{1,0:T(8,128)(2,1)}, u32[]{:S(2)}) copy-start(bf16[128,896]{1,0:T(8,128)(2,1)} %qp_ref.1) | copy-start | bytes 688132
  21.0 1.0 %copy-start.7 = (bf16[128,896]{1,0:T(8,128)(2,1)S(1)}, bf16[128,896]{1,0:T(8,128)(2,1)}, u32[]{:S(2)}) copy-start(bf16[128,896]{1,0:T(8,128)(2,1)} %gp_ref.1) | copy-start | bytes 688132
  33.2 5.0 %copy-start.3 = (bf16[2,256,128]{2,1,0:T(8,128)(2,1)S(1)}, bf16[2,256,128]{2,1,0:T(8,128)(2,1)}, u32[]{:S(2)}) copy-start(bf16[2,256,128]{2,1,0:T(8,128)(2,1)} %kv_ref.5) | copy-start | bytes 393220
  33.2 5.0 %copy-start.5 = (s32[2048]{0:T(1024)S(1)}, s32[2048]{0:T(1024)}, u32[]{:S(2)}) copy-start(s32[2048]{0:T(1024)} %param.11) | copy-start | bytes 24580
  33.2 16.0 %all-to-all-start.1 = ((bf16[32,2,32,128]{3,2,1,0:T(8,128)(2,1)}), bf16[32,2,32,128]{3,2,1,0:T(8,128)(2,1)S(1)}, u32[]{:S(2)}, u32[]{:S(2)}) async-start(bf16[32,2,32,128]{3,2,1,0:T(8,128)(2,1)} %get-tuple-element.32), calls=%async_computation.1 | async-start | bytes 1048576 | tf_op jit(solution)/shard_map/all_to_all | solution.py:322
  40.7 6.2 %collective-permute-start.2 = (bf16[2,64,128]{2,1,0:T(8,128)(2,1)S(1)}, bf16[2,64,128]{2,1,0:T(8,128)(2,1)S(1)}, u32[]{:S(2)}, u32[]{:S(2)}) collective-permute-start(bf16[2,64,128]{2,1,0:T(8,128)(2,1)S(1)} %get-tuple-element.35), channel_id=1, source_target_pairs={{4,0},{8,4},{12,8},{16,12},{20,16},{24,20},{28,24},{5,1},{9,5},{13... | collective-permute-start | bytes 98312 | tf_op jit(solution)/shard_map/ppermute | solution.py:329

commit v4 on v3

--- a/solution.py
+++ b/solution.py
@@ -58,18 +58,18 @@
         out_ref[:, :, t * D : (t + 1) * D] = total.astype(BF)
 
 
-def local_parts(segs_ref, prior_ref, kv_ref, q_ref, g_ref):
+def local_parts(segs_ref, lkv_ref, q_ref, g_ref):
     half = q_ref.shape[0] // 2
     start = pl.multiple_of(lax.axis_index(GROUP) * 2 * half, 2 * half)
     before = segs_ref[:, pl.ds(pl.multiple_of(jnp.maximum(start - half, 0), half), half)]
-    before = jnp.where(start > 0, before, -1)[:, half - BACK :]
-    segs = jnp.concatenate([before, segs_ref[:, pl.ds(start, 2 * half)]], 1).astype(F)
+    before = jnp.where(start > 0, before, -1.0)[:, half - BACK :]
+    segs = jnp.concatenate([before, segs_ref[:, pl.ds(start, 2 * half)]], 1)
     by_key = jnp.broadcast_to(segs, (half, segs.shape[1])).T
     for i in range(2):
         rows = slice(i * half, (i + 1) * half)
         span = slice(i * half, i * half + half + BACK)
-        k = jnp.concatenate([prior_ref[0], kv_ref[0]], 0)[span]
-        v = jnp.concatenate([prior_ref[1], kv_ref[1]], 0)[span]
+        k = lkv_ref[0, span]
+        v = lkv_ref[1, span]
         behind = lax.broadcasted_iota(jnp.int32, (half + BACK, half), 0) - lax.broadcasted_iota(
             jnp.int32, (half + BACK, half), 1
         )
@@ -81,9 +81,9 @@
         yield rows, k, v, q, g, s
 
 
-def local_forward(segs_ref, prior_ref, kv_ref, q_ref, g_ref, stat_ref):
+def local_forward(segs_ref, lkv_ref, q_ref, g_ref, stat_ref):
     heads = q_ref.shape[1] // D
-    for rows, k, v, q, g, s in local_parts(segs_ref, prior_ref, kv_ref, q_ref, g_ref):
+    for rows, k, v, q, g, s in local_parts(segs_ref, lkv_ref, q_ref, g_ref):
         m = jnp.max(s, 0, keepdims=True)
         p = jnp.exp2((s - m) * SCALE2)
         total = jnp.sum(p, 0, keepdims=True)
@@ -96,12 +96,12 @@
 
 
 def local_backward(
-    segs_ref, prior_ref, kv_ref, q_ref, g_ref, stat_ref, fs_ref, o1_ref, dq1_ref,
+    segs_ref, lkv_ref, q_ref, g_ref, stat_ref, fs_ref, o1_ref, dq1_ref,
     back_ref, rest_ref, dkv_ref, o_ref, dq_ref,
 ):
     heads = q_ref.shape[1] // D
     terms = []
-    for rows, k, v, q, g, s in local_parts(segs_ref, prior_ref, kv_ref, q_ref, g_ref):
+    for rows, k, v, q, g, s in local_parts(segs_ref, lkv_ref, q_ref, g_ref):
         m = jnp.concatenate([stat_ref[h, 0:1, rows] for h in range(heads)], 1)
         f = jnp.concatenate([fs_ref[h, 0:1, rows] for h in range(heads)], 1)
         delta = jnp.concatenate([fs_ref[h, 1:2, rows] for h in range(heads)], 1)
@@ -296,14 +296,16 @@
 
     prior = lax.ppermute(tail, GROUP, [(i, i + 1) for i in range(groups - 1)])
 
-    own, prior = lax.optimization_barrier((own, prior))
+    lkv = jnp.concatenate([prior, resp_kv], 1)
+    segs = resp_segs.astype(F).reshape(1, -1)
+    own, lkv, segs = lax.optimization_barrier((own, lkv, segs))
     other = lax.ppermute(own, "core", [(0, 1), (1, 0)])
 
     width = resp_q.shape[1]
     heads = width // D
     rows_all = resp_dev + prompt_dev
     work = 2 * D * heads
-    near = (resp_segs.reshape(1, -1), prior, resp_kv, resp_q, grad_resp_out)
+    near = (segs, lkv, resp_q, grad_resp_out)
     (stats,) = call(local_forward, [shape(heads, 8, resp_dev, dtype=F)], near, work * 2 * 192 * resp_dev)
     wide = (resp_dev, width)
     out1, prompt_out, dq1, grad_prompt_q, factors, terms = call(

time: 50.4 us -> 48.5 us (0.962)
  local copies, waits for them, and re-layouts: 2.8 us -> 0.03 us
  waiting for transfers between devices: 8.07 us -> 9.29 us
    unnamed x16 -> x12, local copies, waits for them, and re-layouts: 2.03 us -> 0.03 us
    slice x1, local copies, waits for them, and re-layouts: 0.77 us -> 0.01 us  [local(): tail = held_kv[:, resp_dev - BACK:]]
    all_to_all x1, waiting for transfers between devices: 1.3 us -> 2.01 us  [local(): own = lax.all_to_all(to_send, ('chip', 'tensor'), 0, 0, tiled=True)]
    ppermute x1, waiting for transfers between devices: 0.01 us -> 0.51 us  [local(): other = lax.ppermute(own, 'core', [(0, 1), (1, 0)])]
  transfers between devices with their start and end apart: 5 -> 5, of which waited for: 4 -> 5; matrix products, arithmetic and copies ran while one was open for 3% -> 1% of each run, Pallas kernels for 6% -> 7%
where the time goes in v4:
time: 48.5 us; the launch traced here: 48.1 us
  starting transfers between devices  20.8 us (43%)
  Pallas kernels  16.6 us (34%)
  waiting for transfers between devices  9.29 us (19%)
  between operations  0.75 us (2%)
  other arithmetic  0.64 us (1%)
    pallas_call x4, Pallas kernels, call(): pl.pallas_call(body, in_specs=[vmem] * len(operands), out_specs=[vmem] *...  15 us
    all_to_all x1, starting transfers between devices, local(): own = lax.all_to_all(to_send, ('chip', 'tensor'), 0, 0, tiled=True)  7.73 us
    all_to_all x1, starting transfers between devices, local(): arrived = lax.all_to_all(terms, both, 0, 0, tiled=True)  4.52 us
    ppermute x1, starting transfers between devices, local(): prior = lax.ppermute(tail, GROUP, [(i, i + 1) for i in range(groups - 1)])  4.39 us
    ppermute x1, waiting for transfers between devices, local(): later = lax.ppermute(back, GROUP, [(i, i - 1) for i in range(1, groups)])  4.07 us
    ppermute x1, starting transfers between devices, local(): later = lax.ppermute(back, GROUP, [(i, i - 1) for i in range(1, groups)])  2.11 us
    ppermute x1, starting transfers between devices, local(): other = lax.ppermute(own, 'core', [(0, 1), (1, 0)])  2.02 us
    all_to_all x1, waiting for transfers between devices, local(): own = lax.all_to_all(to_send, ('chip', 'tensor'), 0, 0, tiled=True)  2.01 us
  transfers between devices with their start and end apart: 5, of which 5 were waited for; matrix products, arithmetic and copies ran while one was open for 1% of the time, Pallas kernels for 7%

profile of v4, /device:TPU:1, one launch (start us, length us, event | category | flops | bytes accessed | tf_op | source)
XLA Modules:
  0.0 48.1 jit_solution(5134971129340466418)
XLA Ops:
  0.6 0.0 copy-start.4
  0.6 0.0 copy-start.5
  0.7 1.6 %spread.1 = bf16[16,2,32,128]{3,2,1,0:T(8,128)(2,1)} custom-call(bf16[2,32,512]{2,1,0:T(8,128)(2,1)} %kv_ref.1), custom_call_target="tpu_custom_call" | custom-call | bytes 262144 | tf_op jit(solution)/shard_map/spread/pallas_call | solution.py:284
  2.3 0.0 copy-start
  2.3 0.0 copy-start.1
  2.3 7.7 %all-to-all-start = ((bf16[16,2,32,128]{3,2,1,0:T(8,128)(2,1)}), bf16[16,2,32,128]{3,2,1,0:T(8,128)(2,1)S(1)}, u32[]{:S(2)}, u32[]{:S(2)}) async-start(bf16[16,2,32,128]{3,2,1,0:T(8,128)(2,1)} %spread.1), calls=%async_computation | async-start | bytes 524288 | tf_op jit(solution)/shard_map/all_to_all | solution.py:295
  10.0 0.0 copy-done.4
  10.1 4.4 %collective-permute-start = (bf16[2,64,128]{2,1,0:T(8,128)(2,1)S(1)}, bf16[2,64,128]{2,1,0:T(8,128)(2,1)S(1)}, u32[]{:S(2)}, u32[]{:S(2)}) collective-permute-start(bf16[2,64,128]{2,1,0:T(8,128)(2,1)S(1)} %slice.3), channel_id=1, source_target_pairs={{0,4},{4,8},{8,12},{12,16},{16,20},{20,24},{24,28},{1,5},{5,9},{9,... | collective-permute-start | bytes 98312 | tf_op jit(solution)/shard_map/ppermute | solution.py:297
  14.5 0.0 copy-done.5
  14.5 1.0 %collective-permute-done = bf16[2,64,128]{2,1,0:T(8,128)(2,1)S(1)} collective-permute-done((bf16[2,64,128]{2,1,0:T(8,128)(2,1)S(1)}, bf16[2,64,128]{2,1,0:T(8,128)(2,1)S(1)}, u32[]{:S(2)}, u32[]{:S(2)}) %collective-permute-start) | collective-permute-done | bytes 32800 | tf_op jit(solution)/shard_map/ppermute | solution.py:297
  15.5 2.0 %all-to-all-done.own_ref = bf16[16,2,32,128]{3,2,1,0:T(8,128)(2,1)S(1)} async-done(((bf16[16,2,32,128]{3,2,1,0:T(8,128)(2,1)}), bf16[16,2,32,128]{3,2,1,0:T(8,128)(2,1)S(1)}, u32[]{:S(2)}, u32[]{:S(2)}) %all-to-all-start) | async-done | bytes 262176 | tf_op jit(solution)/shard_map/all_to_all | solution.py:295
  17.5 0.0 copy-start.2
  17.5 0.0 copy-start.3
  17.5 2.0 %collective-permute-start.1 = (bf16[16,2,32,128]{3,2,1,0:T(8,128)(2,1)S(1)}, bf16[16,2,32,128]{3,2,1,0:T(8,128)(2,1)S(1)}, u32[]{:S(2)}, u32[]{:S(2)}) collective-permute-start(bf16[16,2,32,128]{3,2,1,0:T(8,128)(2,1)S(1)} %all-to-all-done.own_ref), channel_id=1, source_target_pairs={{0,4},{4,0},{1,5},{5,1},{2,6},{6,2},{3,7},{7,3},{8,12},{12,8},{9,1... | collective-permute-start | bytes 786440 | tf_op jit(solution)/shard_map/ppermute | solution.py:302
  19.5 0.0 copy-done
  19.5 0.0 copy-done.1
  19.5 0.6 %local_forward.1.stat_ref = f32[7,8,256]{2,1,0:T(8,128)S(1)} custom-call(f32[1,2048]{1,0:T(1,128)S(1)} %bitcast.1, bf16[2,320,128]{2,1,0:T(8,128)(2,1)S(1)} %pad_maximum_fusion.lkv_ref, bf16[256,896]{1,0:T(8,128)(2,1)S(1)} %copy-done, bf16[256,896]{1,0:T(8,128)(2,1)S(1)} %copy-done.1), custom_call_target="tpu_custom_call" | custom-call | flops 176160768 | bytes 4194304 | tf_op jit(solution)/shard_map/local_forward/pallas_call | solution.py:260
  20.2 0.5 %collective-permute-done.1.other_ref = bf16[16,2,32,128]{3,2,1,0:T(8,128)(2,1)S(1)} collective-permute-done((bf16[16,2,32,128]{3,2,1,0:T(8,128)(2,1)S(1)}, bf16[16,2,32,128]{3,2,1,0:T(8,128)(2,1)S(1)}, u32[]{:S(2)}, u32[]{:S(2)}) %collective-permute-start.1) | collective-permute-done | bytes 262176 | tf_op jit(solution)/shard_map/ppermute | solution.py:302
  20.7 0.0 copy-done.2
  20.7 0.0 copy-done.3
  20.7 11.1 %prefix_attention.1 = (bf16[256,896]{1,0:T(8,128)(2,1)S(1)}, bf16[128,896]{1,0:T(8,128)(2,1)}, bf16[256,896]{1,0:T(8,128)(2,1)S(1)}, bf16[128,896]{1,0:T(8,128)(...) custom-call(bf16[16,2,32,128]{3,2,1,0:T(8,128)(2,1)S(1)} %all-to-all-done.own_ref, ...), custom_call_target="tpu_custom_call" | custom-call | flops 4227858432 | bytes 4194304 | tf_op jit(solution)/shard_map/prefix_attention/pallas_call | solution.py:260
  31.8 4.5 %all-to-all-start.1 = ((bf16[32,2,32,128]{3,2,1,0:T(8,128)(2,1)}), bf16[32,2,32,128]{3,2,1,0:T(8,128)(2,1)S(1)}, u32[]{:S(2)}, u32[]{:S(2)}) async-start(bf16[32,2,32,128]{3,2,1,0:T(8,128)(2,1)} %get-tuple-element.34), calls=%async_computation.1 | async-start | bytes 1048576 | tf_op jit(solution)/shard_map/all_to_all | solution.py:324
  36.3 2.5 %local_backward.1 = (bf16[2,64,128]{2,1,0:T(8,128)(2,1)S(1)}, f32[2,64,128]{2,1,0:T(8,128)S(1)}, bf16[2,256,128]{2,1,0:T(8,128)(2,1)}, bf16[256,896]{1,0:T(8,128)(2,1)}, bf16[256,896]{1,0:T(8,128)(2,1)}) custom-call(f32[1,2048]{1,0:T(1,128)S(1)} %bitcast.2, bf16[2,320,128]{2,1,0:T(8,128)(2,1)S(1)} %pad_maximum_fusion.lkv_ref, bf16[256,896]{1,0:T(8,128)(2,1)S(1)} %copy-done, ...), custom_call_target="tpu_custom_call" | custom-call | flops 440401920 | bytes 4194304 | tf_op jit(solution)/shard_map/local_backward/pallas_call | solution.py:260
  38.8 2.1 %collective-permute-start.2 = (bf16[2,64,128]{2,1,0:T(8,128)(2,1)S(1)}, bf16[2,64,128]{2,1,0:T(8,128)(2,1)S(1)}, u32[]{:S(2)}, u32[]{:S(2)}) collective-permute-start(bf16[2,64,128]{2,1,0:T(8,128)(2,1)S(1)} %get-tuple-element.37), channel_id=1, source_target_pairs={{4,0},{8,4},{12,8},{16,12},{20,16},{24,20},{28,24},{5,1},{9,5},{13... | collective-permute-start | bytes 98312 | tf_op jit(solution)/shard_map/ppermute | solution.py:331
  41.0 4.1 %collective-permute-done.2 = bf16[2,64,128]{2,1,0:T(8,128)(2,1)S(1)} collective-permute-done((bf16[2,64,128]{2,1,0:T(8,128)(2,1)S(1)}, bf16[2,64,128]{2,1,0:T(8,128)(2,1)S(1)}, u32[]{:S(2)}, u32[]{:S(2)}) %collective-permute-start.2) | collective-permute-done | bytes 32800 | tf_op jit(solution)/shard_map/ppermute | solution.py:331
  45.0 0.6 %fusion = bf16[2,256,128]{2,1,0:T(8,128)(2,1)} fusion(bf16[2,256,128]{2,1,0:T(8,128)(2,1)} %get-tuple-element.35, f32[2,64,128]{2,1,0:T(8,128)S(1)} %get-tuple-element.36, bf16[2,64,128]{2,1,0:T(8,128)(2,1)S(1)} %collective-permute-done.2), kind=kLoop, calls=%fused_computation.2 | loop fusion | flops 49152 | bytes 131072 | tf_op jit(solution)/shard_map/dynamic_update_slice | solution.py:332
  45.7 1.7 %all-to-all-done.1.in_ref = bf16[32,2,32,128]{3,2,1,0:T(8,128)(2,1)S(1)} async-done(((bf16[32,2,32,128]{3,2,1,0:T(8,128)(2,1)}), bf16[32,2,32,128]{3,2,1,0:T(8,128)(2,1)S(1)}, u32[]{:S(2)}, u32[]{:S(2)}) %all-to-all-start.1) | async-done | bytes 524320 | tf_op jit(solution)/shard_map/all_to_all | solution.py:324
  47.4 0.7 %gathered_sum.1 = bf16[2,32,512]{2,1,0:T(8,128)(2,1)} custom-call(bf16[32,2,32,128]{3,2,1,0:T(8,128)(2,1)S(1)} %all-to-all-done.1.in_ref), custom_call_target="tpu_custom_call" | custom-call | flops 1048576 | bytes 4194304 | tf_op jit(solution)/shard_map/gathered_sum/pallas_call | solution.py:260
  (3 shorter events, 0.0 us)
Async XLA Ops:
  0.6 9.4 %copy-start.4 = (bf16[2,256,128]{2,1,0:T(8,128)(2,1)S(1)}, bf16[2,256,128]{2,1,0:T(8,128)(2,1)}, u32[]{:S(2)}) copy-start(bf16[2,256,128]{2,1,0:T(8,128)(2,1)} %param.10) | copy-start | bytes 393220
  0.6 13.8 %copy-start.5 = (s32[2048]{0:T(1024)S(1)}, s32[2048]{0:T(1024)}, u32[]{:S(2)}) copy-start(s32[2048]{0:T(1024)} %param.11) | copy-start | bytes 24580
  2.3 17.2 %copy-start = (bf16[256,896]{1,0:T(8,128)(2,1)S(1)}, bf16[256,896]{1,0:T(8,128)(2,1)}, u32[]{:S(2)}) copy-start(bf16[256,896]{1,0:T(8,128)(2,1)} %q_ref.3) | copy-start | bytes 1376260
  2.3 17.2 %copy-start.1 = (bf16[256,896]{1,0:T(8,128)(2,1)S(1)}, bf16[256,896]{1,0:T(8,128)(2,1)}, u32[]{:S(2)}) copy-start(bf16[256,896]{1,0:T(8,128)(2,1)} %g_ref.3) | copy-start | bytes 1376260
  2.3 15.2 %all-to-all-start = ((bf16[16,2,32,128]{3,2,1,0:T(8,128)(2,1)}), bf16[16,2,32,128]{3,2,1,0:T(8,128)(2,1)S(1)}, u32[]{:S(2)}, u32[]{:S(2)}) async-start(bf16[16,2,32,128]{3,2,1,0:T(8,128)(2,1)} %spread.1), calls=%async_computation | async-start | bytes 524288 | tf_op jit(solution)/shard_map/all_to_all | solution.py:295
  10.1 5.4 %collective-permute-start = (bf16[2,64,128]{2,1,0:T(8,128)(2,1)S(1)}, bf16[2,64,128]{2,1,0:T(8,128)(2,1)S(1)}, u32[]{:S(2)}, u32[]{:S(2)}) collective-permute-start(bf16[2,64,128]{2,1,0:T(8,128)(2,1)S(1)} %slice.3), channel_id=1, source_target_pairs={{0,4},{4,8},{8,12},{12,16},{16,20},{20,24},{24,28},{1,5},{5,9},{9,... | collective-permute-start | bytes 98312 | tf_op jit(solution)/shard_map/ppermute | solution.py:297
  17.5 3.2 %copy-start.2 = (bf16[128,896]{1,0:T(8,128)(2,1)S(1)}, bf16[128,896]{1,0:T(8,128)(2,1)}, u32[]{:S(2)}) copy-start(bf16[128,896]{1,0:T(8,128)(2,1)} %qp_ref.1) | copy-start | bytes 688132
  17.5 3.2 %copy-start.3 = (bf16[128,896]{1,0:T(8,128)(2,1)S(1)}, bf16[128,896]{1,0:T(8,128)(2,1)}, u32[]{:S(2)}) copy-start(bf16[128,896]{1,0:T(8,128)(2,1)} %gp_ref.1) | copy-start | bytes 688132
  17.5 3.2 %collective-permute-start.1 = (bf16[16,2,32,128]{3,2,1,0:T(8,128)(2,1)S(1)}, bf16[16,2,32,128]{3,2,1,0:T(8,128)(2,1)S(1)}, u32[]{:S(2)}, u32[]{:S(2)}) collective-permute-start(bf16[16,2,32,128]{3,2,1,0:T(8,128)(2,1)S(1)} %all-to-all-done.own_ref), channel_id=1, source_target_pairs={{0,4},{4,0},{1,5},{5,1},{2,6},{6,2},{3,7},{7,3},{8,12},{12,8},{9,1... | collective-permute-start | bytes 786440 | tf_op jit(solution)/shard_map/ppermute | solution.py:302
  31.8 15.6 %all-to-all-start.1 = ((bf16[32,2,32,128]{3,2,1,0:T(8,128)(2,1)}), bf16[32,2,32,128]{3,2,1,0:T(8,128)(2,1)S(1)}, u32[]{:S(2)}, u32[]{:S(2)}) async-start(bf16[32,2,32,128]{3,2,1,0:T(8,128)(2,1)} %get-tuple-element.34), calls=%async_computation.1 | async-start | bytes 1048576 | tf_op jit(solution)/shard_map/all_to_all | solution.py:324
  38.8 6.2 %collective-permute-start.2 = (bf16[2,64,128]{2,1,0:T(8,128)(2,1)S(1)}, bf16[2,64,128]{2,1,0:T(8,128)(2,1)S(1)}, u32[]{:S(2)}, u32[]{:S(2)}) collective-permute-start(bf16[2,64,128]{2,1,0:T(8,128)(2,1)S(1)} %get-tuple-element.37), channel_id=1, source_target_pairs={{4,0},{8,4},{12,8},{16,12},{20,16},{24,20},{28,24},{5,1},{9,5},{13... | collective-permute-start | bytes 98312 | tf_op jit(solution)/shard_map/ppermute | solution.py:331

commit v5 on v4

--- a/solution.py
+++ b/solution.py
@@ -84,8 +84,8 @@
 def local_forward(segs_ref, lkv_ref, q_ref, g_ref, stat_ref):
     heads = q_ref.shape[1] // D
     for rows, k, v, q, g, s in local_parts(segs_ref, lkv_ref, q_ref, g_ref):
-        m = jnp.max(s, 0, keepdims=True)
-        p = jnp.exp2((s - m) * SCALE2)
+        m = jnp.max(s, 0, keepdims=True) * SCALE2
+        p = jnp.exp2(s * SCALE2 - m)
         total = jnp.sum(p, 0, keepdims=True)
         mix = jnp.sum(p * mm(v, g, NT), 0, keepdims=True)
         for h in range(heads):
@@ -105,7 +105,7 @@
         m = jnp.concatenate([stat_ref[h, 0:1, rows] for h in range(heads)], 1)
         f = jnp.concatenate([fs_ref[h, 0:1, rows] for h in range(heads)], 1)
         delta = jnp.concatenate([fs_ref[h, 1:2, rows] for h in range(heads)], 1)
-        wf = jnp.exp2((s - m) * SCALE2) * f
+        wf = jnp.exp2(s * SCALE2 - m) * f
         w = wf.astype(BF)
         ds = (wf * (mm(v, g, NT) - delta)).astype(BF)
         terms.append((mm(ds, q, NN) * SCALE, mm(w, g, NN)))
@@ -129,7 +129,7 @@
 def prefix_attention(
     own_ref, other_ref, stat_ref, qr_ref, gr_ref, qp_ref, gp_ref,
     or_ref, op_ref, dqr_ref, dqp_ref, fs_ref, terms_ref,
-    k_s, v_s, kt_s, vt_s, s_s, d_s, acck, accv,
+    k_s, v_s, kk_s, kt_s, vt_s, s_s, d_s, acck, accv,
 ):
     heads = qr_ref.shape[1] // D
     keys = k_s.shape[0]
@@ -141,6 +141,10 @@
             at = pl.ds(pl.multiple_of((2 * x + c) * each, each), each)
             k_s[at, :] = ref[4 * x : 4 * x + 4, 0].reshape(each, D)
             v_s[at, :] = ref[4 * x : 4 * x + 4, 1].reshape(each, D)
+    scaled = k_s[...].astype(F) * SCALE2
+    high = scaled.astype(BF)
+    kk_s[:, :D] = high
+    kk_s[:, D:] = (scaled - high.astype(F)).astype(BF)
     kt_s[...] = k_s[...].T
     vt_s[...] = v_s[...].T
     first = lax.axis_index(GROUP) * qp_ref.shape[0]
@@ -169,7 +173,7 @@
             held[u] = {"q": load(qr_ref, qp_ref, unit), "g": load(gr_ref, gp_ref, unit)}
         d = held[u]
         at = slice(k0, k0 + CHUNK)
-        s = mm(k_s[at, :], d["q"], NT)
+        s = mm(kk_s[at, :], jnp.concatenate([d["q"], d["q"]], 1), NT)
         if unit[-1][1] is None:
             cut = [s[:, i * 128 : i * 128 + 128] for i in range(len(unit))]
             seen = ahead <= first - k0
@@ -189,10 +193,9 @@
             m = jnp.max(d["m"], 0, keepdims=True)
             d["m"] = by_block(unit, m, lambda h, r, x: jnp.maximum(x, stat_ref[h, 0:1, r]))
             peak = by_block(unit, d["m"], lambda h, r, x: stat_ref[h, 0:1, r])
-            d["f"] = jnp.exp2((peak - d["m"]) * SCALE2)
-            d["m"] = d["m"] * SCALE2
+            d["f"] = jnp.exp2(peak - d["m"])
         at = slice(k0, k0 + CHUNK)
-        p = jnp.exp2(s_s[u % slots, at, cols] * SCALE2 - d["m"])
+        p = jnp.exp2(s_s[u % slots, at, cols] - d["m"])
         s_s[u % slots, at, cols] = p
         total = fold(p, jnp.sum)
         mix = fold(p * d_s[u % slots, at, cols], jnp.sum)
@@ -316,7 +319,7 @@
         ],
         (own, other, stats, resp_q, grad_resp_out, prompt_q, grad_prompt_out),
         work * 6 * keys * rows_all,
-        [vm((keys, D), BF), vm((keys, D), BF), vm((D, keys), BF), vm((D, keys), BF)]
+        [vm((keys, D), BF), vm((keys, D), BF), vm((keys, 2 * D), BF), vm((D, keys), BF), vm((D, keys), BF)]
         + [vm((3, keys, UNIT * 128), F)] * 2
         + [vm((keys, D), F)] * 2,
         24,

time: 48.5 us -> 48 us (0.990)
  no operation moved by 1% of the time
where the time goes in v5:
time: 48 us; the launch traced here: 47.6 us
  starting transfers between devices  20.8 us (43%)
  Pallas kernels  16.2 us (34%)
  waiting for transfers between devices  9.22 us (19%)
  between operations  0.75 us (2%)
  other arithmetic  0.64 us (1%)
    pallas_call x4, Pallas kernels, call(): pl.pallas_call(body, in_specs=[vmem] * len(operands), out_specs=[vmem] *...  14.6 us
    all_to_all x1, starting transfers between devices, local(): own = lax.all_to_all(to_send, ('chip', 'tensor'), 0, 0, tiled=True)  7.73 us
    all_to_all x1, starting transfers between devices, local(): arrived = lax.all_to_all(terms, both, 0, 0, tiled=True)  4.5 us
    ppermute x1, starting transfers between devices, local(): prior = lax.ppermute(tail, GROUP, [(i, i + 1) for i in range(groups - 1)])  4.39 us
    ppermute x1, waiting for transfers between devices, local(): later = lax.ppermute(back, GROUP, [(i, i - 1) for i in range(1, groups)])  4.06 us
    ppermute x1, starting transfers between devices, local(): later = lax.ppermute(back, GROUP, [(i, i - 1) for i in range(1, groups)])  2.13 us
    ppermute x1, starting transfers between devices, local(): other = lax.ppermute(own, 'core', [(0, 1), (1, 0)])  2.02 us
    all_to_all x1, waiting for transfers between devices, local(): own = lax.all_to_all(to_send, ('chip', 'tensor'), 0, 0, tiled=True)  2.01 us
  transfers between devices with their start and end apart: 5, of which 5 were waited for; matrix products, arithmetic and copies ran while one was open for 1% of the time, Pallas kernels for 7%

profile of v5, /device:TPU:1, one launch (start us, length us, event | category | flops | bytes accessed | tf_op | source)
XLA Modules:
  0.0 47.6 jit_solution(3677802890699261312)
XLA Ops:
  0.6 0.0 copy-start.4
  0.6 0.0 copy-start.5
  0.7 1.6 %spread.1 = bf16[16,2,32,128]{3,2,1,0:T(8,128)(2,1)} custom-call(bf16[2,32,512]{2,1,0:T(8,128)(2,1)} %kv_ref.1), custom_call_target="tpu_custom_call" | custom-call | bytes 262144 | tf_op jit(solution)/shard_map/spread/pallas_call | solution.py:287
  2.3 0.0 copy-start
  2.3 0.0 copy-start.1
  2.3 7.7 %all-to-all-start = ((bf16[16,2,32,128]{3,2,1,0:T(8,128)(2,1)}), bf16[16,2,32,128]{3,2,1,0:T(8,128)(2,1)S(1)}, u32[]{:S(2)}, u32[]{:S(2)}) async-start(bf16[16,2,32,128]{3,2,1,0:T(8,128)(2,1)} %spread.1), calls=%async_computation | async-start | bytes 524288 | tf_op jit(solution)/shard_map/all_to_all | solution.py:298
  10.0 0.0 copy-done.4
  10.1 4.4 %collective-permute-start = (bf16[2,64,128]{2,1,0:T(8,128)(2,1)S(1)}, bf16[2,64,128]{2,1,0:T(8,128)(2,1)S(1)}, u32[]{:S(2)}, u32[]{:S(2)}) collective-permute-start(bf16[2,64,128]{2,1,0:T(8,128)(2,1)S(1)} %slice.3), channel_id=1, source_target_pairs={{0,4},{4,8},{8,12},{12,16},{16,20},{20,24},{24,28},{1,5},{5,9},{9,... | collective-permute-start | bytes 98312 | tf_op jit(solution)/shard_map/ppermute | solution.py:300
  14.5 0.0 copy-done.5
  14.5 1.0 %collective-permute-done = bf16[2,64,128]{2,1,0:T(8,128)(2,1)S(1)} collective-permute-done((bf16[2,64,128]{2,1,0:T(8,128)(2,1)S(1)}, bf16[2,64,128]{2,1,0:T(8,128)(2,1)S(1)}, u32[]{:S(2)}, u32[]{:S(2)}) %collective-permute-start) | collective-permute-done | bytes 32800 | tf_op jit(solution)/shard_map/ppermute | solution.py:300
  15.5 2.0 %all-to-all-done.own_ref = bf16[16,2,32,128]{3,2,1,0:T(8,128)(2,1)S(1)} async-done(((bf16[16,2,32,128]{3,2,1,0:T(8,128)(2,1)}), bf16[16,2,32,128]{3,2,1,0:T(8,128)(2,1)S(1)}, u32[]{:S(2)}, u32[]{:S(2)}) %all-to-all-start) | async-done | bytes 262176 | tf_op jit(solution)/shard_map/all_to_all | solution.py:298
  17.5 0.0 copy-start.2
  17.5 0.0 copy-start.3
  17.5 2.0 %collective-permute-start.1 = (bf16[16,2,32,128]{3,2,1,0:T(8,128)(2,1)S(1)}, bf16[16,2,32,128]{3,2,1,0:T(8,128)(2,1)S(1)}, u32[]{:S(2)}, u32[]{:S(2)}) collective-permute-start(bf16[16,2,32,128]{3,2,1,0:T(8,128)(2,1)S(1)} %all-to-all-done.own_ref), channel_id=1, source_target_pairs={{0,4},{4,0},{1,5},{5,1},{2,6},{6,2},{3,7},{7,3},{8,12},{12,8},{9,1... | collective-permute-start | bytes 786440 | tf_op jit(solution)/shard_map/ppermute | solution.py:305
  19.5 0.0 copy-done
  19.5 0.0 copy-done.1
  19.5 0.7 %local_forward.1.stat_ref = f32[7,8,256]{2,1,0:T(8,128)S(1)} custom-call(f32[1,2048]{1,0:T(1,128)S(1)} %bitcast.1, bf16[2,320,128]{2,1,0:T(8,128)(2,1)S(1)} %pad_maximum_fusion.lkv_ref, bf16[256,896]{1,0:T(8,128)(2,1)S(1)} %copy-done, bf16[256,896]{1,0:T(8,128)(2,1)S(1)} %copy-done.1), custom_call_target="tpu_custom_call" | custom-call | flops 176160768 | bytes 4194304 | tf_op jit(solution)/shard_map/local_forward/pallas_call | solution.py:263
  20.2 0.4 collective-permute-done.1.other_ref
  20.7 0.0 copy-done.2
  20.7 0.0 copy-done.3
  20.7 10.7 %prefix_attention.1 = (bf16[256,896]{1,0:T(8,128)(2,1)S(1)}, bf16[128,896]{1,0:T(8,128)(2,1)}, bf16[256,896]{1,0:T(8,128)(2,1)S(1)}, bf16[128,896]{1,0:T(8,128)(...) custom-call(bf16[16,2,32,128]{3,2,1,0:T(8,128)(2,1)S(1)} %all-to-all-done.own_ref, ...), custom_call_target="tpu_custom_call" | custom-call | flops 4227858432 | bytes 4194304 | tf_op jit(solution)/shard_map/prefix_attention/pallas_call | solution.py:263
  31.4 4.5 %all-to-all-start.1 = ((bf16[32,2,32,128]{3,2,1,0:T(8,128)(2,1)}), bf16[32,2,32,128]{3,2,1,0:T(8,128)(2,1)S(1)}, u32[]{:S(2)}, u32[]{:S(2)}) async-start(bf16[32,2,32,128]{3,2,1,0:T(8,128)(2,1)} %get-tuple-element.34), calls=%async_computation.1 | async-start | bytes 1048576 | tf_op jit(solution)/shard_map/all_to_all | solution.py:327
  35.9 2.5 %local_backward.1 = (bf16[2,64,128]{2,1,0:T(8,128)(2,1)S(1)}, f32[2,64,128]{2,1,0:T(8,128)S(1)}, bf16[2,256,128]{2,1,0:T(8,128)(2,1)}, bf16[256,896]{1,0:T(8,128)(2,1)}, bf16[256,896]{1,0:T(8,128)(2,1)}) custom-call(f32[1,2048]{1,0:T(1,128)S(1)} %bitcast.2, bf16[2,320,128]{2,1,0:T(8,128)(2,1)S(1)} %pad_maximum_fusion.lkv_ref, bf16[256,896]{1,0:T(8,128)(2,1)S(1)} %copy-done, ...), custom_call_target="tpu_custom_call" | custom-call | flops 440401920 | bytes 4194304 | tf_op jit(solution)/shard_map/local_backward/pallas_call | solution.py:263
  38.4 2.1 %collective-permute-start.2 = (bf16[2,64,128]{2,1,0:T(8,128)(2,1)S(1)}, bf16[2,64,128]{2,1,0:T(8,128)(2,1)S(1)}, u32[]{:S(2)}, u32[]{:S(2)}) collective-permute-start(bf16[2,64,128]{2,1,0:T(8,128)(2,1)S(1)} %get-tuple-element.37), channel_id=1, source_target_pairs={{4,0},{8,4},{12,8},{16,12},{20,16},{24,20},{28,24},{5,1},{9,5},{13... | collective-permute-start | bytes 98312 | tf_op jit(solution)/shard_map/ppermute | solution.py:334
  40.5 4.1 %collective-permute-done.2 = bf16[2,64,128]{2,1,0:T(8,128)(2,1)S(1)} collective-permute-done((bf16[2,64,128]{2,1,0:T(8,128)(2,1)S(1)}, bf16[2,64,128]{2,1,0:T(8,128)(2,1)S(1)}, u32[]{:S(2)}, u32[]{:S(2)}) %collective-permute-start.2) | collective-permute-done | bytes 32800 | tf_op jit(solution)/shard_map/ppermute | solution.py:334
  44.6 0.6 %fusion = bf16[2,256,128]{2,1,0:T(8,128)(2,1)} fusion(bf16[2,256,128]{2,1,0:T(8,128)(2,1)} %get-tuple-element.35, f32[2,64,128]{2,1,0:T(8,128)S(1)} %get-tuple-element.36, bf16[2,64,128]{2,1,0:T(8,128)(2,1)S(1)} %collective-permute-done.2), kind=kLoop, calls=%fused_computation.2 | loop fusion | flops 49152 | bytes 131072 | tf_op jit(solution)/shard_map/dynamic_update_slice | solution.py:335
  45.2 1.7 %all-to-all-done.1.in_ref = bf16[32,2,32,128]{3,2,1,0:T(8,128)(2,1)S(1)} async-done(((bf16[32,2,32,128]{3,2,1,0:T(8,128)(2,1)}), bf16[32,2,32,128]{3,2,1,0:T(8,128)(2,1)S(1)}, u32[]{:S(2)}, u32[]{:S(2)}) %all-to-all-start.1) | async-done | bytes 524320 | tf_op jit(solution)/shard_map/all_to_all | solution.py:327
  46.9 0.7 %gathered_sum.1 = bf16[2,32,512]{2,1,0:T(8,128)(2,1)} custom-call(bf16[32,2,32,128]{3,2,1,0:T(8,128)(2,1)S(1)} %all-to-all-done.1.in_ref), custom_call_target="tpu_custom_call" | custom-call | flops 1048576 | bytes 4194304 | tf_op jit(solution)/shard_map/gathered_sum/pallas_call | solution.py:263
  (3 shorter events, 0.0 us)
Async XLA Ops:
  0.6 9.4 %copy-start.4 = (bf16[2,256,128]{2,1,0:T(8,128)(2,1)S(1)}, bf16[2,256,128]{2,1,0:T(8,128)(2,1)}, u32[]{:S(2)}) copy-start(bf16[2,256,128]{2,1,0:T(8,128)(2,1)} %param.10) | copy-start | bytes 393220
  0.6 13.8 %copy-start.5 = (s32[2048]{0:T(1024)S(1)}, s32[2048]{0:T(1024)}, u32[]{:S(2)}) copy-start(s32[2048]{0:T(1024)} %param.11) | copy-start | bytes 24580
  2.3 17.2 %copy-start = (bf16[256,896]{1,0:T(8,128)(2,1)S(1)}, bf16[256,896]{1,0:T(8,128)(2,1)}, u32[]{:S(2)}) copy-start(bf16[256,896]{1,0:T(8,128)(2,1)} %q_ref.3) | copy-start | bytes 1376260
  2.3 17.2 %copy-start.1 = (bf16[256,896]{1,0:T(8,128)(2,1)S(1)}, bf16[256,896]{1,0:T(8,128)(2,1)}, u32[]{:S(2)}) copy-start(bf16[256,896]{1,0:T(8,128)(2,1)} %g_ref.3) | copy-start | bytes 1376260
  2.3 15.2 %all-to-all-start = ((bf16[16,2,32,128]{3,2,1,0:T(8,128)(2,1)}), bf16[16,2,32,128]{3,2,1,0:T(8,128)(2,1)S(1)}, u32[]{:S(2)}, u32[]{:S(2)}) async-start(bf16[16,2,32,128]{3,2,1,0:T(8,128)(2,1)} %spread.1), calls=%async_computation | async-start | bytes 524288 | tf_op jit(solution)/shard_map/all_to_all | solution.py:298
  10.1 5.4 %collective-permute-start = (bf16[2,64,128]{2,1,0:T(8,128)(2,1)S(1)}, bf16[2,64,128]{2,1,0:T(8,128)(2,1)S(1)}, u32[]{:S(2)}, u32[]{:S(2)}) collective-permute-start(bf16[2,64,128]{2,1,0:T(8,128)(2,1)S(1)} %slice.3), channel_id=1, source_target_pairs={{0,4},{4,8},{8,12},{12,16},{16,20},{20,24},{24,28},{1,5},{5,9},{9,... | collective-permute-start | bytes 98312 | tf_op jit(solution)/shard_map/ppermute | solution.py:300
  17.5 3.2 %copy-start.2 = (bf16[128,896]{1,0:T(8,128)(2,1)S(1)}, bf16[128,896]{1,0:T(8,128)(2,1)}, u32[]{:S(2)}) copy-start(bf16[128,896]{1,0:T(8,128)(2,1)} %qp_ref.1) | copy-start | bytes 688132
  17.5 3.2 %copy-start.3 = (bf16[128,896]{1,0:T(8,128)(2,1)S(1)}, bf16[128,896]{1,0:T(8,128)(2,1)}, u32[]{:S(2)}) copy-start(bf16[128,896]{1,0:T(8,128)(2,1)} %gp_ref.1) | copy-start | bytes 688132
  17.5 3.2 %collective-permute-start.1 = (bf16[16,2,32,128]{3,2,1,0:T(8,128)(2,1)S(1)}, bf16[16,2,32,128]{3,2,1,0:T(8,128)(2,1)S(1)}, u32[]{:S(2)}, u32[]{:S(2)}) collective-permute-start(bf16[16,2,32,128]{3,2,1,0:T(8,128)(2,1)S(1)} %all-to-all-done.own_ref), channel_id=1, source_target_pairs={{0,4},{4,0},{1,5},{5,1},{2,6},{6,2},{3,7},{7,3},{8,12},{12,8},{9,1... | collective-permute-start | bytes 786440 | tf_op jit(solution)/shard_map/ppermute | solution.py:305
  31.4 15.5 %all-to-all-start.1 = ((bf16[32,2,32,128]{3,2,1,0:T(8,128)(2,1)}), bf16[32,2,32,128]{3,2,1,0:T(8,128)(2,1)S(1)}, u32[]{:S(2)}, u32[]{:S(2)}) async-start(bf16[32,2,32,128]{3,2,1,0:T(8,128)(2,1)} %get-tuple-element.34), calls=%async_computation.1 | async-start | bytes 1048576 | tf_op jit(solution)/shard_map/all_to_all | solution.py:327
  38.4 6.2 %collective-permute-start.2 = (bf16[2,64,128]{2,1,0:T(8,128)(2,1)S(1)}, bf16[2,64,128]{2,1,0:T(8,128)(2,1)S(1)}, u32[]{:S(2)}, u32[]{:S(2)}) collective-permute-start(bf16[2,64,128]{2,1,0:T(8,128)(2,1)S(1)} %get-tuple-element.37), channel_id=1, source_target_pairs={{4,0},{8,4},{12,8},{16,12},{20,16},{24,20},{28,24},{5,1},{9,5},{13... | collective-permute-start | bytes 98312 | tf_op jit(solution)/shard_map/ppermute | solution.py:334

commit v6 on v5

--- a/solution.py
+++ b/solution.py
@@ -37,16 +37,18 @@
 
 def spread(kv_ref, out_ref, buffer, sem):
     count = buffer.shape[0]
-    for t in range(count):
-        buffer[t] = kv_ref[:, :, t * D : (t + 1) * D]
+    arrivals = [
+        pltpu.make_async_copy(kv_ref.at[:, :, pl.ds(t * D, D)], buffer.at[t], sem.at[t]) for t in range(count)
+    ]
     copies = [
-        pltpu.make_async_copy(buffer, out_ref.at[i : i + count], sem.at[i // count])
+        pltpu.make_async_copy(buffer, out_ref.at[pl.ds(i, count)], sem.at[count + i // count])
         for i in range(0, out_ref.shape[0], count)
     ]
-    for copy in copies:
-        copy.start()
-    for copy in copies:
-        copy.wait()
+    for group in (arrivals, copies):
+        for copy in group:
+            copy.start()
+        for copy in group:
+            copy.wait()
 
 
 def gathered_sum(in_ref, out_ref):
@@ -229,8 +231,14 @@
         d["dq"] = d["dq"] + dq if k0 else dq
         dv = mm(w, d["g"], NN)
         dk = mm(ds, d["q"], NN)
-        accv[at, :] = accv[at, :] + dv if u else dv
-        acck[at, :] = acck[at, :] + dk if u else dk
+        if u + 1 < len(units):
+            accv[at, :] = accv[at, :] + dv if u else dv
+            acck[at, :] = acck[at, :] + dk if u else dk
+        else:
+            each_block = keys // terms_ref.shape[0]
+            to = slice(k0 // each_block, (k0 + CHUNK) // each_block)
+            terms_ref[to, 0] = ((acck[at, :] + dk) * SCALE).astype(BF).reshape(-1, each_block, D)
+            terms_ref[to, 1] = (accv[at, :] + dv).astype(BF).reshape(-1, each_block, D)
         if k0 + CHUNK == keys:
             o = d["o"].T
             dq = d["dq"].T * SCALE
@@ -250,8 +258,6 @@
             for late, stage in enumerate((scores, raised, products)):
                 if 0 <= i - late < len(units):
                     stage(i - late, k0)
-    terms_ref[:, 0] = (acck[...] * SCALE).astype(BF).reshape(-1, keys // terms_ref.shape[0], D)
-    terms_ref[:, 1] = accv[...].astype(BF).reshape(-1, keys // terms_ref.shape[0], D)
 
 
 def shape(*dims, dtype=BF):
@@ -286,10 +292,11 @@
     vm = pltpu.VMEM
     to_send = pl.pallas_call(
         spread,
-        in_specs=[pl.BlockSpec(memory_space=vm)],
+        in_specs=[pl.BlockSpec(memory_space=pl.ANY)],
         out_specs=pl.BlockSpec(memory_space=pl.ANY),
         out_shape=shape(chips * tensors, 2, rows, D),
-        scratch_shapes=[vm((tensors, 2, rows, D), BF), pltpu.SemaphoreType.DMA((chips,))],
+        scratch_shapes=[vm((tensors, 2, rows, D), BF), pltpu.SemaphoreType.DMA((tensors + chips,))],
+        compiler_params=pltpu.CompilerParams(vmem_limit_bytes=60 * 2**20),
         cost_estimate=pl.CostEstimate(flops=0, bytes_accessed=2**18, transcendentals=0),
         name="spread",
     )(prefix_kv)

time: 48 us -> 48 us (level)
  no operation moved by 1% of the time
where the time goes in v6:
time: 48 us; the launch traced here: 47.6 us
  starting transfers between devices  20.8 us (43%)
  Pallas kernels  16.2 us (34%)
  waiting for transfers between devices  9.22 us (19%)
  between operations  0.75 us (2%)
  other arithmetic  0.64 us (1%)
    pallas_call x4, Pallas kernels, call(): pl.pallas_call(body, in_specs=[vmem] * len(operands), out_specs=[vmem] *...  14.6 us
    all_to_all x1, starting transfers between devices, local(): own = lax.all_to_all(to_send, ('chip', 'tensor'), 0, 0, tiled=True)  7.73 us
    all_to_all x1, starting transfers between devices, local(): arrived = lax.all_to_all(terms, both, 0, 0, tiled=True)  4.5 us
    ppermute x1, starting transfers between devices, local(): prior = lax.ppermute(tail, GROUP, [(i, i + 1) for i in range(groups - 1)])  4.39 us
    ppermute x1, waiting for transfers between devices, local(): later = lax.ppermute(back, GROUP, [(i, i - 1) for i in range(1, groups)])  4.06 us
    ppermute x1, starting transfers between devices, local(): later = lax.ppermute(back, GROUP, [(i, i - 1) for i in range(1, groups)])  2.13 us
    ppermute x1, starting transfers between devices, local(): other = lax.ppermute(own, 'core', [(0, 1), (1, 0)])  2.02 us
    all_to_all x1, waiting for transfers between devices, local(): own = lax.all_to_all(to_send, ('chip', 'tensor'), 0, 0, tiled=True)  2.01 us
  transfers between devices with their start and end apart: 5, of which 5 were waited for; matrix products, arithmetic and copies ran while one was open for 1% of the time, Pallas kernels for 7%

profile of v6, /device:TPU:1, one launch (start us, length us, event | category | flops | bytes accessed | tf_op | source)
XLA Modules:
  0.0 47.6 jit_solution(7774564169262998791)
XLA Ops:
  0.6 0.0 copy-start.4
  0.6 0.0 copy-start.5
  0.7 1.6 %spread.1 = bf16[16,2,32,128]{3,2,1,0:T(8,128)(2,1)} custom-call(bf16[2,32,512]{2,1,0:T(8,128)(2,1)} %kv_ref.1), custom_call_target="tpu_custom_call" | custom-call | bytes 262144 | tf_op jit(solution)/shard_map/spread/pallas_call | solution.py:293
  2.2 0.0 copy-start
  2.2 0.0 copy-start.1
  2.2 7.7 %all-to-all-start = ((bf16[16,2,32,128]{3,2,1,0:T(8,128)(2,1)}), bf16[16,2,32,128]{3,2,1,0:T(8,128)(2,1)S(1)}, u32[]{:S(2)}, u32[]{:S(2)}) async-start(bf16[16,2,32,128]{3,2,1,0:T(8,128)(2,1)} %spread.1), calls=%async_computation | async-start | bytes 524288 | tf_op jit(solution)/shard_map/all_to_all | solution.py:305
  10.0 0.0 copy-done.4
  10.0 4.4 %collective-permute-start = (bf16[2,64,128]{2,1,0:T(8,128)(2,1)S(1)}, bf16[2,64,128]{2,1,0:T(8,128)(2,1)S(1)}, u32[]{:S(2)}, u32[]{:S(2)}) collective-permute-start(bf16[2,64,128]{2,1,0:T(8,128)(2,1)S(1)} %slice.3), channel_id=1, source_target_pairs={{0,4},{4,8},{8,12},{12,16},{16,20},{20,24},{24,28},{1,5},{5,9},{9,... | collective-permute-start | bytes 98312 | tf_op jit(solution)/shard_map/ppermute | solution.py:307
  14.4 0.0 copy-done.5
  14.4 1.0 %collective-permute-done = bf16[2,64,128]{2,1,0:T(8,128)(2,1)S(1)} collective-permute-done((bf16[2,64,128]{2,1,0:T(8,128)(2,1)S(1)}, bf16[2,64,128]{2,1,0:T(8,128)(2,1)S(1)}, u32[]{:S(2)}, u32[]{:S(2)}) %collective-permute-start) | collective-permute-done | bytes 32800 | tf_op jit(solution)/shard_map/ppermute | solution.py:307
  15.4 2.0 %all-to-all-done.own_ref = bf16[16,2,32,128]{3,2,1,0:T(8,128)(2,1)S(1)} async-done(((bf16[16,2,32,128]{3,2,1,0:T(8,128)(2,1)}), bf16[16,2,32,128]{3,2,1,0:T(8,128)(2,1)S(1)}, u32[]{:S(2)}, u32[]{:S(2)}) %all-to-all-start) | async-done | bytes 262176 | tf_op jit(solution)/shard_map/all_to_all | solution.py:305
  17.4 0.0 copy-start.2
  17.4 0.0 copy-start.3
  17.4 2.0 %collective-permute-start.1 = (bf16[16,2,32,128]{3,2,1,0:T(8,128)(2,1)S(1)}, bf16[16,2,32,128]{3,2,1,0:T(8,128)(2,1)S(1)}, u32[]{:S(2)}, u32[]{:S(2)}) collective-permute-start(bf16[16,2,32,128]{3,2,1,0:T(8,128)(2,1)S(1)} %all-to-all-done.own_ref), channel_id=1, source_target_pairs={{0,4},{4,0},{1,5},{5,1},{2,6},{6,2},{3,7},{7,3},{8,12},{12,8},{9,1... | collective-permute-start | bytes 786440 | tf_op jit(solution)/shard_map/ppermute | solution.py:312
  19.5 0.0 copy-done
  19.5 0.0 copy-done.1
  19.5 0.7 %local_forward.1.stat_ref = f32[7,8,256]{2,1,0:T(8,128)S(1)} custom-call(f32[1,2048]{1,0:T(1,128)S(1)} %bitcast.1, bf16[2,320,128]{2,1,0:T(8,128)(2,1)S(1)} %pad_maximum_fusion.lkv_ref, bf16[256,896]{1,0:T(8,128)(2,1)S(1)} %copy-done, bf16[256,896]{1,0:T(8,128)(2,1)S(1)} %copy-done.1), custom_call_target="tpu_custom_call" | custom-call | flops 176160768 | bytes 4194304 | tf_op jit(solution)/shard_map/local_forward/pallas_call | solution.py:269
  20.2 0.5 collective-permute-done.1.other_ref
  20.6 0.0 copy-done.2
  20.6 0.0 copy-done.3
  20.6 10.7 %prefix_attention.1 = (bf16[256,896]{1,0:T(8,128)(2,1)S(1)}, bf16[128,896]{1,0:T(8,128)(2,1)}, bf16[256,896]{1,0:T(8,128)(2,1)S(1)}, bf16[128,896]{1,0:T(8,128)(...) custom-call(bf16[16,2,32,128]{3,2,1,0:T(8,128)(2,1)S(1)} %all-to-all-done.own_ref, ...), custom_call_target="tpu_custom_call" | custom-call | flops 4227858432 | bytes 4194304 | tf_op jit(solution)/shard_map/prefix_attention/pallas_call | solution.py:269
  31.3 4.5 %all-to-all-start.1 = ((bf16[32,2,32,128]{3,2,1,0:T(8,128)(2,1)}), bf16[32,2,32,128]{3,2,1,0:T(8,128)(2,1)S(1)}, u32[]{:S(2)}, u32[]{:S(2)}) async-start(bf16[32,2,32,128]{3,2,1,0:T(8,128)(2,1)} %get-tuple-element.34), calls=%async_computation.1 | async-start | bytes 1048576 | tf_op jit(solution)/shard_map/all_to_all | solution.py:334
  35.8 2.5 %local_backward.1 = (bf16[2,64,128]{2,1,0:T(8,128)(2,1)S(1)}, f32[2,64,128]{2,1,0:T(8,128)S(1)}, bf16[2,256,128]{2,1,0:T(8,128)(2,1)}, bf16[256,896]{1,0:T(8,128)(2,1)}, bf16[256,896]{1,0:T(8,128)(2,1)}) custom-call(f32[1,2048]{1,0:T(1,128)S(1)} %bitcast.2, bf16[2,320,128]{2,1,0:T(8,128)(2,1)S(1)} %pad_maximum_fusion.lkv_ref, bf16[256,896]{1,0:T(8,128)(2,1)S(1)} %copy-done, ...), custom_call_target="tpu_custom_call" | custom-call | flops 440401920 | bytes 4194304 | tf_op jit(solution)/shard_map/local_backward/pallas_call | solution.py:269
  38.3 2.1 %collective-permute-start.2 = (bf16[2,64,128]{2,1,0:T(8,128)(2,1)S(1)}, bf16[2,64,128]{2,1,0:T(8,128)(2,1)S(1)}, u32[]{:S(2)}, u32[]{:S(2)}) collective-permute-start(bf16[2,64,128]{2,1,0:T(8,128)(2,1)S(1)} %get-tuple-element.37), channel_id=1, source_target_pairs={{4,0},{8,4},{12,8},{16,12},{20,16},{24,20},{28,24},{5,1},{9,5},{13... | collective-permute-start | bytes 98312 | tf_op jit(solution)/shard_map/ppermute | solution.py:341
  40.5 4.1 %collective-permute-done.2 = bf16[2,64,128]{2,1,0:T(8,128)(2,1)S(1)} collective-permute-done((bf16[2,64,128]{2,1,0:T(8,128)(2,1)S(1)}, bf16[2,64,128]{2,1,0:T(8,128)(2,1)S(1)}, u32[]{:S(2)}, u32[]{:S(2)}) %collective-permute-start.2) | collective-permute-done | bytes 32800 | tf_op jit(solution)/shard_map/ppermute | solution.py:341
  44.5 0.6 %fusion = bf16[2,256,128]{2,1,0:T(8,128)(2,1)} fusion(bf16[2,256,128]{2,1,0:T(8,128)(2,1)} %get-tuple-element.35, f32[2,64,128]{2,1,0:T(8,128)S(1)} %get-tuple-element.36, bf16[2,64,128]{2,1,0:T(8,128)(2,1)S(1)} %collective-permute-done.2), kind=kLoop, calls=%fused_computation.2 | loop fusion | flops 49152 | bytes 131072 | tf_op jit(solution)/shard_map/dynamic_update_slice | solution.py:342
  45.2 1.7 %all-to-all-done.1.in_ref = bf16[32,2,32,128]{3,2,1,0:T(8,128)(2,1)S(1)} async-done(((bf16[32,2,32,128]{3,2,1,0:T(8,128)(2,1)}), bf16[32,2,32,128]{3,2,1,0:T(8,128)(2,1)S(1)}, u32[]{:S(2)}, u32[]{:S(2)}) %all-to-all-start.1) | async-done | bytes 524320 | tf_op jit(solution)/shard_map/all_to_all | solution.py:334
  46.9 0.7 %gathered_sum.1 = bf16[2,32,512]{2,1,0:T(8,128)(2,1)} custom-call(bf16[32,2,32,128]{3,2,1,0:T(8,128)(2,1)S(1)} %all-to-all-done.1.in_ref), custom_call_target="tpu_custom_call" | custom-call | flops 1048576 | bytes 4194304 | tf_op jit(solution)/shard_map/gathered_sum/pallas_call | solution.py:269
  (3 shorter events, 0.0 us)
Async XLA Ops:
  0.6 9.4 %copy-start.4 = (bf16[2,256,128]{2,1,0:T(8,128)(2,1)S(1)}, bf16[2,256,128]{2,1,0:T(8,128)(2,1)}, u32[]{:S(2)}) copy-start(bf16[2,256,128]{2,1,0:T(8,128)(2,1)} %param.10) | copy-start | bytes 393220
  0.6 13.8 %copy-start.5 = (s32[2048]{0:T(1024)S(1)}, s32[2048]{0:T(1024)}, u32[]{:S(2)}) copy-start(s32[2048]{0:T(1024)} %param.11) | copy-start | bytes 24580
  2.2 17.2 %copy-start = (bf16[256,896]{1,0:T(8,128)(2,1)S(1)}, bf16[256,896]{1,0:T(8,128)(2,1)}, u32[]{:S(2)}) copy-start(bf16[256,896]{1,0:T(8,128)(2,1)} %q_ref.3) | copy-start | bytes 1376260
  2.2 17.2 %copy-start.1 = (bf16[256,896]{1,0:T(8,128)(2,1)S(1)}, bf16[256,896]{1,0:T(8,128)(2,1)}, u32[]{:S(2)}) copy-start(bf16[256,896]{1,0:T(8,128)(2,1)} %g_ref.3) | copy-start | bytes 1376260
  2.2 15.2 %all-to-all-start = ((bf16[16,2,32,128]{3,2,1,0:T(8,128)(2,1)}), bf16[16,2,32,128]{3,2,1,0:T(8,128)(2,1)S(1)}, u32[]{:S(2)}, u32[]{:S(2)}) async-start(bf16[16,2,32,128]{3,2,1,0:T(8,128)(2,1)} %spread.1), calls=%async_computation | async-start | bytes 524288 | tf_op jit(solution)/shard_map/all_to_all | solution.py:305
  10.0 5.4 %collective-permute-start = (bf16[2,64,128]{2,1,0:T(8,128)(2,1)S(1)}, bf16[2,64,128]{2,1,0:T(8,128)(2,1)S(1)}, u32[]{:S(2)}, u32[]{:S(2)}) collective-permute-start(bf16[2,64,128]{2,1,0:T(8,128)(2,1)S(1)} %slice.3), channel_id=1, source_target_pairs={{0,4},{4,8},{8,12},{12,16},{16,20},{20,24},{24,28},{1,5},{5,9},{9,... | collective-permute-start | bytes 98312 | tf_op jit(solution)/shard_map/ppermute | solution.py:307
  17.4 3.2 %copy-start.2 = (bf16[128,896]{1,0:T(8,128)(2,1)S(1)}, bf16[128,896]{1,0:T(8,128)(2,1)}, u32[]{:S(2)}) copy-start(bf16[128,896]{1,0:T(8,128)(2,1)} %qp_ref.1) | copy-start | bytes 688132
  17.4 3.2 %copy-start.3 = (bf16[128,896]{1,0:T(8,128)(2,1)S(1)}, bf16[128,896]{1,0:T(8,128)(2,1)}, u32[]{:S(2)}) copy-start(bf16[128,896]{1,0:T(8,128)(2,1)} %gp_ref.1) | copy-start | bytes 688132
  17.4 3.2 %collective-permute-start.1 = (bf16[16,2,32,128]{3,2,1,0:T(8,128)(2,1)S(1)}, bf16[16,2,32,128]{3,2,1,0:T(8,128)(2,1)S(1)}, u32[]{:S(2)}, u32[]{:S(2)}) collective-permute-start(bf16[16,2,32,128]{3,2,1,0:T(8,128)(2,1)S(1)} %all-to-all-done.own_ref), channel_id=1, source_target_pairs={{0,4},{4,0},{1,5},{5,1},{2,6},{6,2},{3,7},{7,3},{8,12},{12,8},{9,1... | collective-permute-start | bytes 786440 | tf_op jit(solution)/shard_map/ppermute | solution.py:312
  31.3 15.5 %all-to-all-start.1 = ((bf16[32,2,32,128]{3,2,1,0:T(8,128)(2,1)}), bf16[32,2,32,128]{3,2,1,0:T(8,128)(2,1)S(1)}, u32[]{:S(2)}, u32[]{:S(2)}) async-start(bf16[32,2,32,128]{3,2,1,0:T(8,128)(2,1)} %get-tuple-element.34), calls=%async_computation.1 | async-start | bytes 1048576 | tf_op jit(solution)/shard_map/all_to_all | solution.py:334
  38.3 6.2 %collective-permute-start.2 = (bf16[2,64,128]{2,1,0:T(8,128)(2,1)S(1)}, bf16[2,64,128]{2,1,0:T(8,128)(2,1)S(1)}, u32[]{:S(2)}, u32[]{:S(2)}) collective-permute-start(bf16[2,64,128]{2,1,0:T(8,128)(2,1)S(1)} %get-tuple-element.37), channel_id=1, source_target_pairs={{4,0},{8,4},{12,8},{16,12},{20,16},{24,20},{28,24},{5,1},{9,5},{13... | collective-permute-start | bytes 98312 | tf_op jit(solution)/shard_map/ppermute | solution.py:341
